TPU v7x, 256 devices: a whole 4x4x8 slice. The times are simulated.
256 devices in a mesh: inst: 64 (over x_lo, z, y), tp: 4 (over x_hi, core).
Axes of the slice: x: 4 (x_hi: 2, x_lo: 2; x = x_hi * 2 + x_lo), y: 4, z: 8, core: 2. Of those that a mesh axis runs over, the one named last changes fastest.
Arguments:
- res_keys: bfloat16 [384, 4, 1024, 128], P('inst', 'tp'), may hold values from -12 to 12, as said below
- res_values: bfloat16 [384, 4, 1024, 128], P('inst', 'tp'), may hold values from -6 to 6
- pool_keys: bfloat16 [1024, 4, 128, 128], P('inst', 'tp'), may hold values from -12 to 12
- pool_values: bfloat16 [1024, 4, 128, 128], P('inst', 'tp'), may hold values from -6 to 6
- queries: bfloat16 [640, 32, 4, 128], P('inst', 'tp'), may hold values from -25 to 25
- new_keys: bfloat16 [640, 4, 4, 128], P('inst', 'tp'), may hold values from -6 to 6
- new_values: bfloat16 [640, 4, 4, 128], P('inst', 'tp'), may hold values from -6 to 6
- res_len: int32 [384], replicated, may hold values from 1 to 1024, as said below
- new_len: int32 [256], replicated, may hold values from 1921 to 2048, as said below
- page_source: int32 [64, 64], replicated, may hold values from 0 to 63, as said below
- page_index: int32 [64, 64], replicated, may hold values from 0 to 15
- partner_bit: int32 [64], replicated, may hold values from 0 to 1, as said below
- migrate_out: int32 [64], replicated, may hold values from 1 to 2
- out_weight: bfloat16 [4096, 4096], P('tp'), may hold values from -0.09375 to 0.09375
Outputs:
- mixed: bfloat16 [3072, 4096], P('inst', 'tp')
Inputs may be any that keep to these rules, and one draw needn't show every extreme that they name: `res_keys`: scores of the cache reach far beyond one in some rows. `res_len`: 1024 is reached by some request. `new_len`: 2048 is reached by some request; every page of a new request is live. `page_source`: each destination takes at most 2 pages from one source, and exactly 2 from some source. `partner_bit`: below 2, the same for all instances of an aligned group of 2 ** 2, so the pairs form a perfect matching inside each group.
All inputs are finite; a program needn't handle non-finite values.
Results may differ from a plain program's by a relative error of at most 0.008.
Values may be sent and summed in bfloat16 or wider, within the bound.
A program may use at most 128 MiB of HBM per device.

v0:
```python
import math

import jax
import jax.numpy as jnp
from jax import lax
from jax.sharding import PartitionSpec as P

MIG = 2
MATCH_BITS = 2


def partner(value, axis, distance):
    mask = 2**distance
    pairs = [(source, source ^ mask) for source in range(lax.axis_size(axis))]
    return lax.ppermute(value, axis, pairs)


def attend(cache_keys, values, length, queries, fresh_keys, fresh_values):
    heads_kv, context, head_dim = cache_keys.shape
    group_size = queries.shape[0] // heads_kv
    step_count = queries.shape[1]
    score_scale = 1.0 / math.sqrt(head_dim)
    grouped = queries.reshape(heads_kv, group_size, step_count, head_dim)
    old_scores = (
        jnp.einsum("kgtd,kcd->kgtc", grouped, cache_keys, preferred_element_type=jnp.float32)
        * score_scale
    )
    new_scores = (
        jnp.einsum("kgtd,ksd->kgts", grouped, fresh_keys, preferred_element_type=jnp.float32)
        * score_scale
    )
    old_live = (jnp.arange(context, dtype=jnp.int32) < length)[None, None, None, :]
    positions = jnp.arange(step_count, dtype=jnp.int32)
    new_live = (positions[None, :] <= positions[:, None])[None, None]
    old_scores = jnp.where(old_live, old_scores, -jnp.inf)
    new_scores = jnp.where(new_live, new_scores, -jnp.inf)
    peak_score = jnp.maximum(jnp.max(old_scores, axis=-1), jnp.max(new_scores, axis=-1))[..., None]
    old_exp = jnp.exp(old_scores - peak_score)
    new_exp = jnp.exp(new_scores - peak_score)
    weight_total = jnp.sum(old_exp, axis=-1, keepdims=True) + jnp.sum(
        new_exp, axis=-1, keepdims=True
    )
    old_weight = (old_exp / weight_total).astype(jnp.bfloat16)
    new_weight = (new_exp / weight_total).astype(jnp.bfloat16)
    attended = jnp.einsum("kgtc,kcd->kgtd", old_weight, values, preferred_element_type=jnp.float32)
    attended = attended + jnp.einsum(
        "kgts,ksd->kgtd", new_weight, fresh_values, preferred_element_type=jnp.float32
    )
    return attended.reshape(heads_kv * group_size, step_count, head_dim).astype(jnp.bfloat16)


def per_device(
    res_keys,
    res_values,
    pool_keys,
    pool_values,
    queries,
    new_keys,
    new_values,
    res_len,
    new_len,
    page_source,
    page_index,
    partner_bit,
    migrate_out,
    out_weight,
):
    inst_count = lax.axis_size("inst")
    here_index = lax.axis_index("inst")
    res_here = res_keys.shape[0]
    new_here = queries.shape[0] - res_here
    in_pages = page_source.shape[1]
    pages_each = in_pages // new_here
    capacity = max(1, 2 * in_pages // inst_count)
    bf_zero = jnp.zeros((), jnp.bfloat16)
    same_source = page_source[:, :, None] == page_source[:, None, :]
    positions = jnp.arange(in_pages, dtype=jnp.int32)
    earlier = positions[None, :] < positions[:, None]
    source_rank = jnp.sum((same_source & earlier[None]).astype(jnp.int32), axis=2)
    from_here = page_source == here_index
    slot_ids = jnp.arange(capacity, dtype=jnp.int32)
    picked = from_here[:, None, :] & (source_rank[:, None, :] == slot_ids[None, :, None])
    chosen_page = jnp.sum(jnp.where(picked, page_index[:, None, :], 0), axis=2)
    filled = jnp.any(picked, axis=2)
    arrived = page_source[here_index] * capacity + source_rank[here_index]
    own_new_len = lax.dynamic_slice_in_dim(new_len, here_index * new_here, new_here, 0)
    fresh_queries = queries[res_here:]
    fresh_keys = new_keys[res_here:]
    fresh_values = new_values[res_here:]
    filled_mask = filled[:, :, None, None, None]
    send_keys = jnp.where(filled_mask, pool_keys[chosen_page], bf_zero)
    send_values = jnp.where(filled_mask, pool_values[chosen_page], bf_zero)
    got_keys, got_values = (
        lax.all_to_all(send_keys, "inst", split_axis=0, concat_axis=0, tiled=True),
        lax.all_to_all(send_values, "inst", split_axis=0, concat_axis=0, tiled=True),
    )

    def arrange(page_block):
        heads_kv, block_len, head_dim = page_block.shape[2:]
        stacked = page_block.reshape((inst_count * capacity, heads_kv, block_len, head_dim))[
            arrived
        ]
        stacked = stacked.reshape(new_here, pages_each, heads_kv, block_len, head_dim).transpose(
            0, 2, 1, 3, 4
        )
        return stacked.reshape(new_here, heads_kv, pages_each * block_len, head_dim)

    new_out = jax.vmap(attend)(
        arrange(got_keys), arrange(got_values), own_new_len, fresh_queries, fresh_keys, fresh_values
    )
    own_len = lax.dynamic_slice_in_dim(res_len, here_index * res_here, res_here, 0)
    own_out = jax.vmap(attend)(
        res_keys,
        res_values,
        own_len,
        queries[:res_here],
        new_keys[:res_here],
        new_values[:res_here],
    )
    hand_here = migrate_out[here_index]
    pair_bit = partner_bit[here_index]
    partner_index = jnp.bitwise_xor(here_index, jnp.left_shift(jnp.int32(1), pair_bit))
    hand_there = migrate_out[partner_index]
    mig_start = res_here - MIG
    outgoing = own_out[mig_start:]
    guest_out = outgoing
    for bit_number in range(MATCH_BITS):
        incoming = partner(outgoing, "inst", bit_number)
        guest_out = jnp.where(pair_bit == bit_number, incoming, guest_out)
    guest_mask = jnp.arange(MIG, dtype=jnp.int32) >= MIG - hand_there
    guest_out = jnp.where(guest_mask[:, None, None, None], guest_out, bf_zero)
    keep_mask = jnp.arange(res_here, dtype=jnp.int32) < res_here - hand_here
    own_out = jnp.where(keep_mask[:, None, None, None], own_out, bf_zero)
    all_slots = jnp.concatenate([own_out, guest_out, new_out], axis=0)
    flat_rows = all_slots.transpose(0, 2, 1, 3).reshape(
        all_slots.shape[0] * all_slots.shape[2], all_slots.shape[1] * all_slots.shape[3]
    )
    partial_sum = jnp.dot(flat_rows, out_weight, preferred_element_type=jnp.float32)
    return lax.psum_scatter(partial_sum, "tp", scatter_dimension=1, tiled=True).astype(jnp.bfloat16)


def solution(mesh):
    in_specs = (
        P("inst", "tp", None, None),
        P("inst", "tp", None, None),
        P("inst", "tp", None, None),
        P("inst", "tp", None, None),
        P("inst", "tp", None, None),
        P("inst", "tp", None, None),
        P("inst", "tp", None, None),
        P(),
        P(),
        P(),
        P(),
        P(),
        P(),
        P("tp", None),
    )
    out_specs = P("inst", "tp")
    return jax.shard_map(
        per_device, mesh=mesh, in_specs=in_specs, out_specs=out_specs, check_vma=False
    )
```

profile of v0, /device:TPU:1, one launch (start us, length us, event | category | flops | bytes accessed | tf_op | source)
XLA Modules:
  0.0 289.4 jit_solution(17879328342978935038)
XLA Ops:
  6.6 2.7 convert_reduce_fusion
  9.3 0.8 broadcast_compare_fusion
  10.1 0.9 select_reduce_fusion
  11.4 4.2 %gather_fusion = bf16[128,128,128]{2,1,0:T(8,128)(2,1)} fusion(bf16[16,128,128]{2,1,0:T(8,128)(2,1)} %bitcast.96, s32[1024]{0:T(1024)S(1)} %pad_clamp_fusion.1), kind=kCustom, calls=%fused_computation | custom fusion | bytes 8389120 | tf_op jit(solution)/shard_map/gather | solution.py:91
  15.6 3.1 %gather_fusion.2 = bf16[128,128,128]{2,1,0:T(8,128)(2,1)} fusion(bf16[16,128,128]{2,1,0:T(8,128)(2,1)S(1)} %bitcast.97, s32[1024]{0:T(1024)S(1)} %pad_clamp_fusion.1), kind=kCustom, calls=%fused_computation.2 | custom fusion | bytes 8389120 | tf_op jit(solution)/shard_map/gather | solution.py:92
  18.6 5.1 %broadcast_select_fusion.1 = (bf16[64,2,1,128,128]{4,3,1,2,0:T(8,128)(2,1)}, bf16[64,2,1,128,128]{4,3,1,2,0:T(8,128)(2,1)S(1)}) fusion(bf16[64,2,1,128,128]{4,3,1,2,0:T(8,128)(2,1)} %bitcast.98, pred[64,2]{1,0:T(8,128)(4,1)S(1)} %copy.39, bf16[64,2,1,128,128]{4,3,1,2,0:T(8,128)(2,1)} %bitcast.99), kind=kLoop, calls=%fused_computation.5 | loop fusion | flops 4194304 | bytes 16777344 | tf_op jit(solution)/shard_map/jit(_where)/select_n | solution.py:91
  23.7 105.9 %all_to_all.10 = bf16[64,2,1,128,128]{4,3,1,2,0:T(8,128)(2,1)} all-to-all(bf16[64,2,1,128,128]{4,3,1,2,0:T(8,128)(2,1)S(1)} %get-tuple-element.6), channel_id=1, replica_groups=mesh['inst'=64,'tp'=4] {'inst'}, dimensions={0} | all-to-all | bytes 8388608 | tf_op jit(solution)/shard_map/all_to_all | solution.py:95
  129.7 9.5 %all-to-all-start = ((bf16[64,2,1,128,128]{4,3,1,2,0:T(8,128)(2,1)}), bf16[64,2,1,128,128]{4,3,1,2,0:T(8,128)(2,1)}, u32[]{:S(2)}, u32[]{:S(2)}) async-start(bf16[64,2,1,128,128]{4,3,1,2,0:T(8,128)(2,1)} %get-tuple-element.5), calls=%async_computation | async-start | bytes 8388608 | tf_op jit(solution)/shard_map/all_to_all | solution.py:94
  139.3 0.6 dynamic_slice.23
  140.6 0.7 fusion.43
  141.9 0.8 dynamic_slice.22
  142.8 0.3 fusion.47
  143.1 0.7 fusion.46
  144.4 1.8 broadcast_select_fusion.2
  146.3 2.5 collective-permute-start
  149.8 0.7 fusion.42
  152.3 4.4 %gather_fusion.3 = bf16[64,128,128]{2,1,0:T(8,128)(2,1)} fusion(bf16[128,128,128]{2,1,0:T(8,128)(2,1)} %bitcast.100, s32[1024]{0:T(1024)S(1)} %pad_clamp_fusion), kind=kCustom, calls=%fused_computation.3 | custom fusion | bytes 4194560 | tf_op jit(solution)/shard_map/gather | solution.py:100
  156.7 74.7 %all-to-all-done = bf16[64,2,1,128,128]{4,3,1,2,0:T(8,128)(2,1)} async-done(((bf16[64,2,1,128,128]{4,3,1,2,0:T(8,128)(2,1)}), bf16[64,2,1,128,128]{4,3,1,2,0:T(8,128)(2,1)}, u32[]{:S(2)}, u32[]{:S(2)}) %all-to-all-start) | async-done | bytes 4194336 | tf_op jit(solution)/shard_map/all_to_all | solution.py:94
  231.4 4.4 %gather_fusion.1 = bf16[64,128,128]{2,1,0:T(8,128)(2,1)} fusion(bf16[128,128,128]{2,1,0:T(8,128)(2,1)} %bitcast.22, s32[1024]{0:T(1024)S(1)} %pad_clamp_fusion), kind=kCustom, calls=%fused_computation.1 | custom fusion | bytes 4194560 | tf_op jit(solution)/shard_map/gather | solution.py:100
  235.7 2.6 fusion.44
  238.7 0.5 fusion.23
  239.4 5.8 %fusion.26 = f32[48,4096]{1,0:T(8,128)} fusion(bf16[1024,4096]{1,0:T(8,128)(2,1)} %param.27, bf16[6,8,8,128]{3,2,1,0:T(8,128)(2,1)S(1)} %bitcast.103), kind=kOutput, calls=%fused_computation.33 | convolution fusion | flops 402653184 | bytes 9273344 | tf_op jit(solution)/shard_map/dot_general | solution.py:138
  245.3 35.7 %reduce-scatter.2.cloned.1.call-done = f32[48,1024]{1,0:T(8,128)} async-done(((f32[48,4096]{1,0:T(8,128)}), f32[48,1024]{1,0:T(8,128)}) %reduce-scatter.2.cloned.1.call-update) | async-done | bytes 196624 | tf_op jit(solution)/shard_map/reduce_scatter | solution.py:139
  281.0 1.6 convert_element_type.35
  (53 shorter events, 2.7 us)
Async XLA Ops:
  6.5 136.6 %copy-start = (bf16[6,1,1024,128]{3,2,1,0:T(8,128)(2,1)S(1)}, bf16[6,1,1024,128]{3,2,1,0:T(8,128)(2,1)}, u32[]{:S(2)}) copy-start(bf16[6,1,1024,128]{3,2,1,0:T(8,128)(2,1)} %param.14) | copy-start | bytes 4718596
  11.4 4.2 %copy-start.1 = (bf16[16,1,128,128]{3,2,1,0:T(8,128)(2,1)S(1)}, bf16[16,1,128,128]{3,2,1,0:T(8,128)(2,1)}, u32[]{:S(2)}) copy-start(bf16[16,1,128,128]{3,2,1,0:T(8,128)(2,1)} %param.17) | copy-start | bytes 1572868
  129.7 9.6 %copy-start.8 = (s32[64]{0:T(128)S(1)}, s32[64]{0:T(128)}, u32[]{:S(2)}) copy-start(s32[64]{0:T(128)} %param.25) | copy-start | bytes 772
  129.7 10.9 %copy-start.3 = (bf16[10,8,4,128]{3,2,1,0:T(4,128)(2,1)S(1)}, bf16[10,8,4,128]{3,2,1,0:T(4,128)(2,1)}, u32[]{:S(2)}) copy-start(bf16[10,8,4,128]{3,2,1,0:T(4,128)(2,1)} %param.18) | copy-start | bytes 245764
  129.7 10.9 %copy-start.4 = (s32[64]{0:T(128)S(1)}, s32[64]{0:T(128)}, u32[]{:S(2)}) copy-start(s32[64]{0:T(128)} %param.26) | copy-start | bytes 772
  129.7 13.1 %copy-start.5 = (bf16[10,1,4,128]{3,2,1,0:T(4,128)(2,1)S(1)}, bf16[10,1,4,128]{3,2,1,0:T(4,128)(2,1)}, u32[]{:S(2)}) copy-start(bf16[10,1,4,128]{3,2,1,0:T(4,128)(2,1)} %param.19) | copy-start | bytes 30724
  129.7 101.7 %all-to-all-start = ((bf16[64,2,1,128,128]{4,3,1,2,0:T(8,128)(2,1)}), bf16[64,2,1,128,128]{4,3,1,2,0:T(8,128)(2,1)}, u32[]{:S(2)}, u32[]{:S(2)}) async-start(bf16[64,2,1,128,128]{4,3,1,2,0:T(8,128)(2,1)} %get-tuple-element.5), calls=%async_computation | async-start | bytes 8388608 | tf_op jit(solution)/shard_map/all_to_all | solution.py:94
  139.2 5.0 %copy-start.6 = (bf16[10,1,4,128]{3,2,1,0:T(4,128)(2,1)S(1)}, bf16[10,1,4,128]{3,2,1,0:T(4,128)(2,1)}, u32[]{:S(2)}) copy-start(bf16[10,1,4,128]{3,2,1,0:T(4,128)(2,1)} %param.20) | copy-start | bytes 30724
  139.2 141.8 %reduce-scatter.2.cloned.1.call-start = ((), (), s32[]{:S(2)}) async-start(), calls=%async_computation.3 | async-start | bytes 983040 | tf_op jit(solution)/shard_map/reduce_scatter | solution.py:139
  144.4 4.7 %copy-start.7 = (s32[256]{0:T(256)S(1)}, s32[256]{0:T(256)}, u32[]{:S(2)}) copy-start(s32[256]{0:T(256)} %param.22) | copy-start | bytes 3076
  146.3 5.9 %collective-permute-start = (bf16[2,8,4,128]{3,1,2,0:T(8,128)(2,1)S(1)}, bf16[2,8,4,128]{3,1,2,0:T(8,128)(2,1)S(1)}, u32[]{:S(2)}, u32[]{:S(2)}) collective-permute-start(bf16[2,8,4,128]{3,1,2,0:T(8,128)(2,1)S(1)} %slice.38), channel_id=1, source_target_pairs={{0,8},{4,12},{8,0},{12,4},{16,24},{20,28},{24,16},{28,20},{32,40},... | collective-permute-start | bytes 49160 | tf_op jit(solution)/shard_map/ppermute | solution.py:15
  148.8 3.4 %collective-permute-start.1 = (bf16[2,8,4,128]{3,1,2,0:T(8,128)(2,1)S(1)}, bf16[2,8,4,128]{3,1,2,0:T(8,128)(2,1)S(1)}, u32[]{:S(2)}, u32[]{:S(2)}) collective-permute-start(bf16[2,8,4,128]{3,1,2,0:T(8,128)(2,1)S(1)} %slice.38), channel_id=1, source_target_pairs={{0,4},{4,0},{8,12},{12,8},{16,20},{20,16},{24,28},{28,24},{32,36},... | collective-permute-start | bytes 49160 | tf_op jit(solution)/shard_map/ppermute | solution.py:15
  235.7 3.0 %copy-start.2 = (bf16[64,128,128]{2,1,0:T(8,128)(2,1)S(1)}, bf16[64,128,128]{2,1,0:T(8,128)(2,1)}, u32[]{:S(2)}) copy-start(bf16[64,128,128]{2,1,0:T(8,128)(2,1)} %gather_fusion.3) | copy-start | bytes 6291460
Sparse Core Ops, SparseCore 0:
  245.4 35.5 reduce-scatter.1
where the time goes:
time: 290 us; the launch traced here: 289 us
  waiting for transfers between devices  110 us (38%)
  blocking collectives  106 us (37%)
  local copies, waits for them, and re-layouts  18.4 us (6%)
  between operations  16.9 us (6%)
  other arithmetic  12.9 us (4%)
  matrix products  12.5 us (4%)
  starting transfers between devices  12.4 us (4%)
    all_to_all x1, blocking collectives, per_device(): lax.all_to_all(send_values, 'inst', split_axis=0, concat_axis=0, tiled=True)  106 us
    all_to_all x1, waiting for transfers between devices, per_device(): lax.all_to_all(send_keys, 'inst', split_axis=0, concat_axis=0, tiled=True)  74.7 us
    reduce_scatter x1, waiting for transfers between devices, per_device(): lax.psum_scatter(partial_sum, 'tp', scatter_dimension=1, tiled=True)  35.7 us
    all_to_all x1, starting transfers between devices, per_device(): lax.all_to_all(send_keys, 'inst', split_axis=0, concat_axis=0, tiled=True)  9.52 us
    gather x2, local copies, waits for them, and re-layouts, arrange(): page_block.reshape((inst_count * capacity, heads_kv, block_len, head_dim))  8.71 us
    dot_general x1, matrix products, per_device(): jnp.dot(flat_rows, out_weight, preferred_element_type=jnp.float32)  5.83 us
  transfers between devices with their start and end apart: 4, of which 2 were waited for; matrix products, arithmetic and copies ran while one was open for 4% of the time, Pallas kernels for 0%

commit v1 on v0

v1 whole, which is shorter than its diff:
```python
import math

import jax
import jax.numpy as jnp
from jax import lax
from jax.experimental import pallas as pl
from jax.experimental.pallas import tpu as pltpu
from jax.sharding import PartitionSpec as P

MESH = pl.DeviceIdType.MESH
NX, NZ, NY = 2, 8, 4
PEERS = NX * NY
TP = 4
RES, NEW, MIG = 6, 4, 2
STEPS = 4
ROWS = 32
HD = 128
PAGE = 128
NPAGES = 16
LOW = -1e30
GROUPS = 12
NT = (((1,), (1,)), ((), ()))
NN = (((1,), (0,)), ((), ()))


def mirror(r):
    dx, dy = divmod(r, NY)
    return dx * NY + (NY - dy) % NY


def iota(shape, axis):
    return lax.broadcasted_iota(jnp.int32, shape, axis)


def dot(a, b, dims=NN):
    return lax.dot_general(a, b, dims, preferred_element_type=jnp.float32)


def kernel(
    res_len,
    new_len,
    partner_bit,
    migrate_out,
    page_source,
    page_index,
    queries,
    new_keys,
    new_values,
    res_keys,
    res_values,
    pool_keys,
    pool_values,
    weight,
    out,
    rk,
    rv,
    pk,
    pv,
    wv,
    tab_v,
    tab,
    q1,
    fw,
    q2,
    r1s,
    r1,
    sts,
    st,
    r2s,
    ls,
    fin,
    lf,
    att,
    guest,
    attm,
    xres,
    xnew,
    own1,
    own2,
    rs1s,
    rs1,
    rs2s,
    rs2,
    load_sem,
    q1_send,
    q1_recv,
    q2_send,
    q2_recv,
    r1_send,
    r1_recv,
    st_send,
    st_recv,
    r2_send,
    r2_recv,
    lf_send,
    lf_recv,
    mig_send,
    mig_recv,
    rs1_send,
    rs1_recv,
    rs2_send,
    rs2_recv,
):
    me = lax.axis_index("inst")
    tp = lax.axis_index("tp")
    y = lax.rem(me, NY)
    z = lax.rem(lax.div(me, NY), NZ)
    x = lax.div(me, NY * NZ)
    hi = lax.div(tp, 2)
    core = lax.rem(tp, 2)
    scale = 1.0 / math.sqrt(HD)

    def inst_at(xx, zz, yy):
        return (xx * NZ + zz) * NY + yy

    def plane(r, zz):
        dx, dy = divmod(r, NY)
        return inst_at(lax.rem(x + dx, NX), zz, lax.rem(y + dy, NY))

    def line(zi):
        return inst_at(x, lax.rem(z + zi, NZ), y)

    def tp_peer(o):
        return lax.rem(hi + o // 2, 2) * 2 + lax.rem(core + o % 2, 2)

    def order(i):
        odd = lax.rem(i, 2)
        return lax.rem(odd * lax.div(i + 1, 2) + (1 - odd) * (NZ - lax.div(i, 2)), NZ)

    def remote(src, dst, send, recv, inst, t=tp):
        return pltpu.make_async_remote_copy(
            src_ref=src,
            dst_ref=dst,
            send_sem=send,
            recv_sem=recv,
            device_id=(inst, t),
            device_id_type=MESH,
        )

    def drain(ref, sem):
        pltpu.make_async_copy(ref, ref, sem).wait()

    loads = [
        pltpu.make_async_copy(src, dst, load_sem.at[k])
        for k, (src, dst) in enumerate(
            [
                (res_keys, rk),
                (res_values, rv),
                (pool_keys, pk),
                (pool_values, pv),
                (weight, wv),
            ]
        )
    ]
    for copy in loads:
        copy.start()

    barrier = pltpu.get_barrier_semaphore()
    for zi in range(1, NZ):
        pl.semaphore_signal(barrier, inc=1, device_id=(line(zi), tp), device_id_type=MESH)
    for r in range(1, PEERS):
        pl.semaphore_signal(barrier, inc=1, device_id=(plane(r, z), tp), device_id_type=MESH)
    for o in range(1, TP):
        pl.semaphore_signal(barrier, inc=1, device_id=(me, tp_peer(o)), device_id_type=MESH)
    pl.semaphore_wait(barrier, NZ - 1 + PEERS - 1 + TP - 1)

    seq = [0, 1, 7, 2, 6, 3, 5, 4]
    q1_copies = []
    for i in range(1, NZ):
        zi = seq[i]
        back = seq.index(NZ - zi)
        copy = remote(
            queries.at[pl.ds(RES * ROWS, NEW * ROWS)],
            q1.at[back],
            q1_send.at[i],
            q1_recv.at[back],
            line(zi),
        )
        copy.start()
        q1_copies.append(copy)
    q1[0] = queries[RES * ROWS :, :]

    places = page_source.shape[1]
    count = page_source.shape[0]
    source = page_source[...]
    slot = page_index[...]
    place = iota((count, places), 1)
    lane = iota((count, HD), 1)
    table = jnp.zeros((count, HD), jnp.int32)
    for r in range(PEERS):
        hit = source == plane(r, z)
        first = jnp.min(jnp.where(hit, place, places), axis=1, keepdims=True)
        last = jnp.max(jnp.where(hit, place, -1), axis=1, keepdims=True)
        last = jnp.where(last > first, last, places)
        table = jnp.where(lane == 2 * r, first, table)
        table = jnp.where(lane == 2 * r + 1, last, table)
        if r == 0:
            for c, p in ((0, first), (1, last)):
                page = jnp.max(jnp.where(place == p, slot, 0), axis=1, keepdims=True)
                table = jnp.where(lane == 2 * PEERS + c, page, table)
    tab_v[...] = table
    tab_copy = pltpu.make_async_copy(tab_v, tab, load_sem.at[5])
    tab_copy.start()
    tab_copy.wait()

    def forward(i):
        dest = line(order(i))
        block = [q1[i, pl.ds(n * ROWS, ROWS), :] for n in range(NEW)]
        for r in range(PEERS):
            for c in range(2):
                n = lax.div(tab[dest, 2 * r + c], NPAGES)
                q = lax.select(
                    n == 0,
                    block[0],
                    lax.select(n == 1, block[1], lax.select(n == 2, block[2], block[3])),
                )
                if r == 0:
                    q2[i, 0, pl.ds(c * ROWS, ROWS), :] = q
                else:
                    fw[i, r, pl.ds(c * ROWS, ROWS), :] = q
            if r > 0:
                remote(
                    fw.at[i, r], q2.at[i, mirror(r)], q2_send.at[i], q2_recv.at[i], plane(r, z)
                ).start()

    forward(jnp.int32(0))

    def forward_step(i, carry):
        drain(q1.at[i], q1_recv.at[i])
        forward(i)
        return carry

    lax.fori_loop(1, NZ, forward_step, 0)

    fresh_count = new_keys.shape[0]
    fresh_k = new_keys[...]
    fresh_v = new_values[...]
    diag = iota((ROWS, HD), 0) == lax.rem(iota((ROWS, HD), 1), ROWS)

    def fresh_scores(request, q):
        s = dot(q, fresh_k, NT) * scale
        row = iota((ROWS, fresh_count), 0)
        col = iota((ROWS, fresh_count), 1)
        live = (lax.div(col, STEPS) == request) & (lax.rem(col, STEPS) <= lax.rem(row, STEPS))
        return jnp.where(live, s, LOW)

    def as_row(column):
        return jnp.sum(jnp.where(diag, column, 0.0), axis=0, keepdims=True)

    quarter = lax.div(iota((1, HD), 1), ROWS)
    for n in range(NEW):
        s = fresh_scores(RES + n, queries[pl.ds((RES + n) * ROWS, ROWS), :])
        m = jnp.max(s, axis=1, keepdims=True)
        p = jnp.exp(s - m)
        l = jnp.sum(p, axis=1, keepdims=True)
        fin[n, 8] = (dot(p.astype(jnp.bfloat16), fresh_v) / l).astype(jnp.bfloat16)
        for g in range(9, GROUPS):
            fin[n, g] = jnp.zeros((ROWS, HD), jnp.bfloat16)
        lf[NZ, pl.ds(n, 1), :] = jnp.where(quarter == 0, as_row(m + jnp.log(l)), LOW)

    loads[0].wait()
    loads[1].wait()
    context = rk.shape[1]

    def resident_step(i, carry):
        for half in range(2):
            request = 2 * i + half
            q = queries[pl.ds(pl.multiple_of(request * ROWS, ROWS), ROWS), :]
            s = dot(q, rk[request], NT) * scale
            s = jnp.where(iota((ROWS, context), 1) < res_len[me * RES + request], s, LOW)
            f = fresh_scores(request, q)
            m = jnp.maximum(
                jnp.max(s, axis=1, keepdims=True), jnp.max(f, axis=1, keepdims=True)
            )
            p = jnp.exp(s - m)
            g = jnp.exp(f - m)
            l = jnp.sum(p, axis=1, keepdims=True) + jnp.sum(g, axis=1, keepdims=True)
            o = dot(p.astype(jnp.bfloat16), rv[request]) + dot(g.astype(jnp.bfloat16), fresh_v)
            att[pl.ds(pl.multiple_of(request * ROWS, ROWS), ROWS), :] = (o / l).astype(
                jnp.bfloat16
            )
        return carry

    lax.fori_loop(0, RES // 2, resident_step, 0)
    partners = [
        inst_at(x, z, y + 1 - 2 * lax.rem(y, 2)),
        inst_at(x, z, lax.rem(y + 2, NY)),
    ]
    mig_copies = []
    for bit in range(2):
        copy = remote(
            att.at[pl.ds((RES - MIG) * ROWS, MIG * ROWS)],
            guest.at[bit],
            mig_send.at[bit],
            mig_recv.at[bit],
            partners[bit],
        )
        copy.start()
        mig_copies.append(copy)

    loads[2].wait()
    loads[3].wait()
    low_half = lax.rem(lax.div(iota((1, HD), 1), ROWS), 2) == 0
    tile_row = iota((2 * NEW, HD), 0)
    key_lane = iota((ROWS, PAGE), 1)

    def partial_step(ip, carry):
        tiles = [jnp.full((2 * NEW, HD), LOW, jnp.float32) for _ in range(PEERS)]
        for half in range(2):
            i = 2 * ip + half
            drain(q2.at[i, pl.ds(1, PEERS - 1)], q2_recv.at[i])
            dest_z = lax.rem(z + order(i), NZ)
            for base in range(0, PEERS, 2):
                scores, values, request = [], [], []
                for r in (base, base + 1):
                    dest = plane(r, dest_z)
                    for c in range(2):
                        at = tab[dest, c]
                        page = tab[dest, 2 * PEERS + c]
                        n = lax.div(at, NPAGES)
                        length = new_len[dest * NEW + jnp.minimum(n, NEW - 1)]
                        live = length - lax.rem(at, NPAGES) * PAGE
                        s = dot(q2[i, r, pl.ds(c * ROWS, ROWS), :], pk[page], NT) * scale
                        scores.append(jnp.where(key_lane < live, s, LOW))
                        values.append(pv[page])
                        request.append(n)
                tops = [jnp.max(s, axis=1, keepdims=True) for s in scores]
                exps = [jnp.exp(s - m) for s, m in zip(scores, tops)]
                sums = [jnp.sum(p, axis=1, keepdims=True) for p in exps]
                outs = [
                    (dot(p.astype(jnp.bfloat16), v) / l).astype(jnp.bfloat16)
                    for p, v, l in zip(exps, values, sums)
                ]
                rows = [as_row(m + jnp.log(l)) for m, l in zip(tops, sums)]
                for k, r in enumerate((base, base + 1)):
                    for c in range(2):
                        if r == 0:
                            r1[i, 0, pl.ds(c * ROWS, ROWS), :] = outs[2 * k + c]
                        else:
                            r1s[i, r, pl.ds(c * ROWS, ROWS), :] = outs[2 * k + c]
                    level = jnp.where(low_half, rows[2 * k], rows[2 * k + 1])
                    wanted = jnp.where(low_half, request[2 * k], request[2 * k + 1]) + half * NEW
                    filled = jnp.where(low_half, request[2 * k], request[2 * k + 1]) < NEW
                    tiles[r] = jnp.where((tile_row == wanted) & filled, level, tiles[r])
                    if r > 0:
                        remote(
                            r1s.at[i, r],
                            r1.at[i, mirror(r)],
                            r1_send.at[i],
                            r1_recv.at[i],
                            plane(r, z),
                        ).start()
        for r in range(PEERS):
            if r == 0:
                st[ip, 0] = tiles[0]
            else:
                sts[ip, r] = tiles[r]
                remote(
                    sts.at[ip, r],
                    st.at[ip, mirror(r)],
                    st_send.at[ip],
                    st_recv.at[ip],
                    plane(r, z),
                ).start()
        return carry

    lax.fori_loop(0, NZ // 2, partial_step, 0)

    for copy in mig_copies:
        copy.wait()
    bit = partner_bit[me]
    hand_here = migrate_out[me]
    hand_there = lax.select(bit == 0, migrate_out[partners[0]], migrate_out[partners[1]])
    nothing = jnp.zeros((ROWS, HD), jnp.bfloat16)
    for r in range(RES):
        attm[pl.ds(r * ROWS, ROWS), :] = lax.select(
            r < RES - hand_here, att[pl.ds(r * ROWS, ROWS), :], nothing
        )
    for m in range(MIG):
        came = lax.select(
            bit == 0, guest[0, pl.ds(m * ROWS, ROWS), :], guest[1, pl.ds(m * ROWS, ROWS), :]
        )
        attm[pl.ds((RES + m) * ROWS, ROWS), :] = lax.select(
            m >= MIG - hand_there, came, nothing
        )

    def by_head(values, slots):
        size = slots * ROWS
        row = iota((size, size), 0)
        col = iota((size, size), 1)
        goal = (
            lax.rem(lax.div(row, STEPS), slots) * ROWS
            + lax.div(row, STEPS * slots) * STEPS
            + lax.rem(row, STEPS)
        )
        moved = dot(jnp.where(col == goal, 1.0, 0.0).astype(jnp.bfloat16), values)
        return moved.astype(jnp.bfloat16)

    moved = by_head(attm[...], RES + MIG)
    lead = (RES + MIG) * STEPS
    for h in range(ROWS // STEPS):
        xres[:, pl.ds(h * HD, HD)] = moved[h * lead : (h + 1) * lead]
    loads[4].wait()
    width = out.shape[1]

    def project(rows_ref, sends, send_sem, recv, recv_sem, own):
        copies = []
        for o in (3, 2, 1, 0):
            peer = tp_peer(o)
            part = dot(rows_ref[...], wv[:, pl.ds(pl.multiple_of(peer * width, width), width)])
            if o == 0:
                own[...] = part
            else:
                sends[o] = part.astype(jnp.bfloat16)
                copy = remote(sends.at[o], recv.at[o], send_sem.at[o], recv_sem.at[o], me, peer)
                copy.start()
                copies.append(copy)
        return copies

    rs1_copies = project(xres, rs1s, rs1_send, rs1, rs1_recv, own1)

    low = iota((2 * NEW, HD), 1) < 2 * ROWS

    def merge(ip, home):
        drain(st.at[ip, pl.ds(1, PEERS - 1)], st_recv.at[ip])
        levels = [
            jnp.where(low, st[ip, 2 * q], st[ip, 2 * q + 1]) for q in range(PEERS // 2)
        ]
        m = jnp.maximum(
            jnp.maximum(levels[0], levels[1]), jnp.maximum(levels[2], levels[3])
        )
        m = jnp.maximum(m, pltpu.roll(m, 2 * ROWS, 1))
        m = jnp.maximum(m, pltpu.roll(m, ROWS, 1))
        shares = [jnp.exp(level - m) for level in levels]
        total = (shares[0] + shares[1]) + (shares[2] + shares[3])
        total = total + pltpu.roll(total, 2 * ROWS, 1)
        total = total + pltpu.roll(total, ROWS, 1)
        ls[ip] = m + jnp.log(total)
        shares = [share / total for share in shares]
        for half in range(2):
            i = 2 * ip + half
            drain(r1.at[i, pl.ds(1, PEERS - 1)], r1_recv.at[i])
            blocks = []
            for n in range(NEW):
                k = half * NEW + n
                blocks.append(
                    jnp.concatenate(
                        [jnp.where(diag, share[k : k + 1], 0.0) for share in shares], axis=1
                    )
                )
            mix = jnp.concatenate(blocks, axis=0).astype(jnp.bfloat16)
            merged = dot(mix, r1[i].reshape(PEERS * 2 * ROWS, HD)).astype(jnp.bfloat16)
            if home and half == 0:
                for n in range(NEW):
                    fin[n, 0] = merged[n * ROWS : (n + 1) * ROWS]
                lf[0] = ls[ip]
            else:
                for n in range(NEW):
                    r2s[i, n] = merged[n * ROWS : (n + 1) * ROWS]
                zi = order(i)
                turned = i + 1 - 2 * lax.rem(i + 1, 2)
                back = turned - lax.div(turned, NZ)
                remote(
                    r2s.at[i], fin.at[:, back], r2_send.at[i], r2_recv.at[back], line(zi)
                ).start()
                remote(ls.at[ip], lf.at[back], lf_send.at[i], lf_recv.at[back], line(zi)).start()

    merge(jnp.int32(0), True)

    def merge_step(ip, carry):
        merge(ip, False)
        return carry

    lax.fori_loop(1, NZ // 2, merge_step, 0)

    for i in range(1, NZ):
        drain(lf.at[i], lf_recv.at[i])
        drain(fin.at[:, i], r2_recv.at[i])
    from_odd = [False, False, True, False, True, False, True, True]
    levels = []
    for base in range(0, NZ, 4):
        level = jnp.full((NEW, HD), LOW, jnp.float32)
        for g in range(4):
            i = base + g
            rows = lf[i, pl.ds(NEW if from_odd[i] else 0, NEW), :]
            level = jnp.where(quarter == g, rows, level)
        levels.append(level)
    levels.append(lf[NZ, pl.ds(0, NEW), :])
    m = jnp.maximum(jnp.maximum(levels[0], levels[1]), levels[2])
    m = jnp.maximum(m, pltpu.roll(m, 2 * ROWS, 1))
    m = jnp.maximum(m, pltpu.roll(m, ROWS, 1))
    shares = [jnp.exp(level - m) for level in levels]
    total = shares[0] + shares[1] + shares[2]
    total = total + pltpu.roll(total, 2 * ROWS, 1)
    total = total + pltpu.roll(total, ROWS, 1)
    shares = [share / total for share in shares]
    attended = []
    for n in range(NEW):
        mix = jnp.concatenate(
            [jnp.where(diag, share[n : n + 1], 0.0) for share in shares], axis=1
        ).astype(jnp.bfloat16)
        attended.append(dot(mix, fin[n].reshape(GROUPS * ROWS, HD)))
    moved = by_head(jnp.concatenate(attended, axis=0).astype(jnp.bfloat16), NEW)
    tail = NEW * STEPS
    for h in range(ROWS // STEPS):
        xnew[:, pl.ds(h * HD, HD)] = moved[h * tail : (h + 1) * tail]
    rs2_copies = project(xnew, rs2s, rs2_send, rs2, rs2_recv, own2)

    for copy in rs1_copies:
        copy.wait()
    total = own1[...]
    for o in range(1, TP):
        total = total + rs1[o].astype(jnp.float32)
    out[pl.ds(0, lead), :] = total.astype(jnp.bfloat16)
    for copy in q1_copies:
        copy.wait_send()
    for i in range(NZ):
        drain(fw.at[i, pl.ds(1, PEERS - 1)], q2_send.at[i])
        drain(r1s.at[i, pl.ds(1, PEERS - 1)], r1_send.at[i])
        if i > 0:
            drain(r2s.at[i], r2_send.at[i])
            drain(ls.at[i // 2], lf_send.at[i])
    for ip in range(NZ // 2):
        drain(sts.at[ip, pl.ds(1, PEERS - 1)], st_send.at[ip])
    for copy in rs2_copies:
        copy.wait()
    total = own2[...]
    for o in range(1, TP):
        total = total + rs2[o].astype(jnp.float32)
    out[pl.ds(lead, tail), :] = total.astype(jnp.bfloat16)


def per_device(
    res_keys,
    res_values,
    pool_keys,
    pool_values,
    queries,
    new_keys,
    new_values,
    res_len,
    new_len,
    page_source,
    page_index,
    partner_bit,
    migrate_out,
    out_weight,
):
    bf, f32 = jnp.bfloat16, jnp.float32
    rows = (RES + MIG + NEW) * STEPS
    lead, tail = (RES + MIG) * STEPS, NEW * STEPS
    width = out_weight.shape[1] // TP
    smem = pl.BlockSpec(memory_space=pltpu.SMEM)
    vmem = pl.BlockSpec(memory_space=pltpu.VMEM)
    hbm = pl.BlockSpec(memory_space=pl.ANY)
    dma = pltpu.SemaphoreType.DMA
    depth = out_weight.shape[0]
    scratch = [
        pltpu.VMEM((RES, res_keys.shape[2], HD), bf),
        pltpu.VMEM((RES, res_keys.shape[2], HD), bf),
        pltpu.VMEM((pool_keys.shape[0], PAGE, HD), bf),
        pltpu.VMEM((pool_keys.shape[0], PAGE, HD), bf),
        pltpu.VMEM(out_weight.shape, bf),
        pltpu.VMEM((page_source.shape[0], HD), jnp.int32),
        pltpu.SMEM((page_source.shape[0], HD), jnp.int32),
        pltpu.VMEM((NZ, NEW * ROWS, HD), bf),
        pltpu.VMEM((NZ, PEERS, 2 * ROWS, HD), bf),
        pltpu.VMEM((NZ, PEERS, 2 * ROWS, HD), bf),
        pltpu.VMEM((NZ, PEERS, 2 * ROWS, HD), bf),
        pltpu.VMEM((NZ, PEERS, 2 * ROWS, HD), bf),
        pltpu.VMEM((NZ // 2, PEERS, 2 * NEW, HD), f32),
        pltpu.VMEM((NZ // 2, PEERS, 2 * NEW, HD), f32),
        pltpu.VMEM((NZ, NEW, ROWS, HD), bf),
        pltpu.VMEM((NZ // 2, 2 * NEW, HD), f32),
        pltpu.VMEM((NEW, GROUPS, ROWS, HD), bf),
        pltpu.VMEM((NZ + 1, 2 * NEW, HD), f32),
        pltpu.VMEM((RES * ROWS, HD), bf),
        pltpu.VMEM((2, MIG * ROWS, HD), bf),
        pltpu.VMEM(((RES + MIG) * ROWS, HD), bf),
        pltpu.VMEM((lead, depth), bf),
        pltpu.VMEM((tail, depth), bf),
        pltpu.VMEM((lead, width), f32),
        pltpu.VMEM((tail, width), f32),
        pltpu.VMEM((TP, lead, width), bf),
        pltpu.VMEM((TP, lead, width), bf),
        pltpu.VMEM((TP, tail, width), bf),
        pltpu.VMEM((TP, tail, width), bf),
        dma((6,)),
        dma((NZ,)),
        dma((NZ,)),
        dma((NZ,)),
        dma((NZ,)),
        dma((NZ,)),
        dma((NZ,)),
        dma((NZ // 2,)),
        dma((NZ // 2,)),
        dma((NZ,)),
        dma((NZ,)),
        dma((NZ,)),
        dma((NZ,)),
        dma((2,)),
        dma((2,)),
        dma((TP,)),
        dma((TP,)),
        dma((TP,)),
        dma((TP,)),
    ]
    return pl.pallas_call(
        kernel,
        out_shape=jax.ShapeDtypeStruct((rows, width), bf),
        in_specs=[smem] * 4 + [vmem] * 5 + [hbm] * 5,
        out_specs=vmem,
        scratch_shapes=scratch,
        compiler_params=pltpu.CompilerParams(
            collective_id=0, has_side_effects=True, vmem_limit_bytes=48 * 2**20
        ),
        cost_estimate=pl.CostEstimate(
            flops=10**9, bytes_accessed=16 * 2**20, transcendentals=10**6
        ),
    )(
        res_len,
        new_len,
        partner_bit,
        migrate_out,
        page_source,
        page_index,
        queries.reshape(-1, HD),
        new_keys.reshape(-1, HD),
        new_values.reshape(-1, HD),
        res_keys.reshape(RES, -1, HD),
        res_values.reshape(RES, -1, HD),
        pool_keys.reshape(-1, PAGE, HD),
        pool_values.reshape(-1, PAGE, HD),
        out_weight,
    )


def solution(mesh):
    heads = P("inst", "tp", None, None)
    in_specs = (heads,) * 7 + (P(),) * 6 + (P("tp", None),)
    return jax.shard_map(
        per_device, mesh=mesh, in_specs=in_specs, out_specs=P("inst", "tp"), check_vma=False
    )
```

time: 290 us -> 65.3 us (0.23)
  waiting for transfers between devices: 110 us -> 0 us
  blocking collectives: 106 us -> 0 us
  Pallas kernels: 0 us -> 52.7 us
  between operations: 16.9 us -> 0.02 us
  other arithmetic: 12.9 us -> 0 us
  matrix products: 12.5 us -> 0 us
  starting transfers between devices: 12.4 us -> 0 us
  local copies, waits for them, and re-layouts: 18.4 us -> 12 us
    all_to_all x1 -> x0, blocking collectives: 106 us -> none  [per_device(): lax.all_to_all(send_values, 'inst', split_axis=0, concat_axis=0, tiled=True)]
    all_to_all x1 -> x0, waiting for transfers between devices: 74.7 us -> none  [per_device(): lax.all_to_all(send_keys, 'inst', split_axis=0, concat_axis=0, tiled=True)]
    pallas_call x0 -> x1, Pallas kernels: none -> 52.7 us  [per_device(): pl.pallas_call(kernel, out_shape=jax.ShapeDtypeStruct((rows, width), bf),...]
    reduce_scatter x1 -> x0, waiting for transfers between devices: 35.7 us -> none  [per_device(): lax.psum_scatter(partial_sum, 'tp', scatter_dimension=1, tiled=True)]
    gather x4 -> x0, local copies, waits for them, and re-layouts: 15.9 us -> none  [the longest x2 8.71 us: arrange(): page_block.reshape((inst_count * capacity, heads_kv, block_len, head_dim))]
    dot_general x9 -> x0, matrix products: 12.5 us -> none  [the longest x1 5.83 us: per_device(): jnp.dot(flat_rows, out_weight, preferred_element_type=jnp.float32)]
    unnamed x18 -> x27, local copies, waits for them, and re-layouts: 0.04 us -> 12 us
    all_to_all x1 -> x0, starting transfers between devices: 9.52 us -> none  [per_device(): lax.all_to_all(send_keys, 'inst', split_axis=0, concat_axis=0, tiled=True)]
  transfers between devices with their start and end apart: 4 -> 0, of which waited for: 2 -> 0; matrix products, arithmetic and copies ran while one was open for 4% -> 0% of each run, Pallas kernels for 0% -> 0%
where the time goes in v1:
time: 65.3 us; the launch traced here: 64.7 us
  Pallas kernels  52.7 us (81%)
  local copies, waits for them, and re-layouts  12 us (18%)
    pallas_call x1, Pallas kernels, per_device(): pl.pallas_call(kernel, out_shape=jax.ShapeDtypeStruct((rows, width), bf),...  52.7 us
    unnamed x27, local copies, waits for them, and re-layouts  12 us

profile of v1, /device:TPU:1, one launch (start us, length us, event | category | flops | bytes accessed | tf_op | source)
XLA Modules:
  0.0 64.7 jit_solution(17355306990347282072)
XLA Ops:
  0.0 0.0 copy-start
  0.0 1.4 %copy-done = bf16[6,1,1024,128]{3,2,1,0:T(8,128)(2,1)S(1)} copy-done((bf16[6,1,1024,128]{3,2,1,0:T(8,128)(2,1)S(1)}, bf16[6,1,1024,128]{3,2,1,0:T(8,128)(2,1)}, u32[]{:S(2)}) %copy-start) | copy-done | bytes 1572888
  1.4 0.0 copy-start.1
  1.4 1.4 %copy-done.1 = bf16[6,1,1024,128]{3,2,1,0:T(8,128)(2,1)S(1)} copy-done((bf16[6,1,1024,128]{3,2,1,0:T(8,128)(2,1)S(1)}, bf16[6,1,1024,128]{3,2,1,0:T(8,128)(2,1)}, u32[]{:S(2)}) %copy-start.1) | copy-done | bytes 1572888
  2.8 0.0 copy-start.2
  2.8 1.0 %copy-done.2 = bf16[16,1,128,128]{3,2,1,0:T(8,128)(2,1)S(1)} copy-done((bf16[16,1,128,128]{3,2,1,0:T(8,128)(2,1)S(1)}, bf16[16,1,128,128]{3,2,1,0:T(8,128)(2,1)}, u32[]{:S(2)}) %copy-start.2) | copy-done | bytes 524312
  3.9 0.0 copy-start.3
  3.9 1.0 %copy-done.3 = bf16[16,1,128,128]{3,2,1,0:T(8,128)(2,1)S(1)} copy-done((bf16[16,1,128,128]{3,2,1,0:T(8,128)(2,1)S(1)}, bf16[16,1,128,128]{3,2,1,0:T(8,128)(2,1)}, u32[]{:S(2)}) %copy-start.3) | copy-done | bytes 524312
  4.9 0.0 copy-start.4
  4.9 0.9 %copy-done.4 = bf16[10,8,4,128]{3,2,1,0:T(4,128)(2,1)S(1)} copy-done((bf16[10,8,4,128]{3,2,1,0:T(4,128)(2,1)S(1)}, bf16[10,8,4,128]{3,2,1,0:T(4,128)(2,1)}, u32[]{:S(2)}) %copy-start.4) | copy-done | bytes 81944
  5.8 0.0 copy-start.5
  5.8 0.8 %copy-done.5 = s32[64,64]{1,0:T(8,128)S(1)} copy-done((s32[64,64]{1,0:T(8,128)S(1)}, s32[64,64]{1,0:T(8,128)}, u32[]{:S(2)}) %copy-start.5) | copy-done | bytes 16408
  6.5 0.0 copy-start.6
  6.5 0.8 %copy-done.6 = s32[64,64]{1,0:T(8,128)S(1)} copy-done((s32[64,64]{1,0:T(8,128)S(1)}, s32[64,64]{1,0:T(8,128)}, u32[]{:S(2)}) %copy-start.6) | copy-done | bytes 16408
  7.3 0.0 copy-start.7
  7.3 0.7 %copy-done.7 = bf16[10,1,4,128]{3,2,1,0:T(4,128)(2,1)S(1)} copy-done((bf16[10,1,4,128]{3,2,1,0:T(4,128)(2,1)S(1)}, bf16[10,1,4,128]{3,2,1,0:T(4,128)(2,1)}, u32[]{:S(2)}) %copy-start.7) | copy-done | bytes 10264
  8.0 0.0 copy-start.8
  8.0 0.7 %copy-done.8 = bf16[10,1,4,128]{3,2,1,0:T(4,128)(2,1)S(1)} copy-done((bf16[10,1,4,128]{3,2,1,0:T(4,128)(2,1)S(1)}, bf16[10,1,4,128]{3,2,1,0:T(4,128)(2,1)}, u32[]{:S(2)}) %copy-start.8) | copy-done | bytes 10264
  8.7 0.7 %copy-done.9 = s32[384]{0:T(512)S(1)} copy-done((s32[384]{0:T(512)S(1)}, s32[384]{0:T(512)}, u32[]{:S(2)}) %copy-start.9) | copy-done | bytes 1560
  9.4 0.7 %copy-done.10 = s32[256]{0:T(256)S(1)} copy-done((s32[256]{0:T(256)S(1)}, s32[256]{0:T(256)}, u32[]{:S(2)}) %copy-start.10) | copy-done | bytes 1048
  10.1 0.7 %copy-done.11 = s32[64]{0:T(128)S(1)} copy-done((s32[64]{0:T(128)S(1)}, s32[64]{0:T(128)}, u32[]{:S(2)}) %copy-start.11) | copy-done | bytes 280
  10.7 0.7 %copy-done.12 = s32[64]{0:T(128)S(1)} copy-done((s32[64]{0:T(128)S(1)}, s32[64]{0:T(128)}, u32[]{:S(2)}) %copy-start.12) | copy-done | bytes 280
  11.4 52.7 %shard_map.136 = bf16[48,1024]{1,0:T(8,128)(2,1)S(1)} custom-call(s32[384]{0:T(512)S(1)} %copy-done.9, s32[256]{0:T(256)S(1)} %copy-done.10, s32[64]{0:T(128)S(1)} %copy-done.11, s32[64]{0:T(128)S(1)} %copy-done.12, s32[64,64]{1,0:T(8,128)S(1)} %copy-done.5, s32[64,64]{1,0:T(8,128)S(1)} %copy-done.6, bf16[320,128]{1,0:T(8,128)(2,1)S(1)} %bitcast.11, ...), custom_call_target="tpu_custom_call" | custom-call | flops 1000000000 | bytes 16777216 | tf_op jit(solution)/shard_map/pallas_call | solution.py:608
  64.1 0.6 copy.16
  (4 shorter events, 0.0 us)
Async XLA Ops:
  0.0 1.4 %copy-start = (bf16[6,1,1024,128]{3,2,1,0:T(8,128)(2,1)S(1)}, bf16[6,1,1024,128]{3,2,1,0:T(8,128)(2,1)}, u32[]{:S(2)}) copy-start(bf16[6,1,1024,128]{3,2,1,0:T(8,128)(2,1)} %param.14) | copy-start | bytes 4718596
  1.4 1.4 %copy-start.1 = (bf16[6,1,1024,128]{3,2,1,0:T(8,128)(2,1)S(1)}, bf16[6,1,1024,128]{3,2,1,0:T(8,128)(2,1)}, u32[]{:S(2)}) copy-start(bf16[6,1,1024,128]{3,2,1,0:T(8,128)(2,1)} %param.15) | copy-start | bytes 4718596
  2.8 1.0 %copy-start.2 = (bf16[16,1,128,128]{3,2,1,0:T(8,128)(2,1)S(1)}, bf16[16,1,128,128]{3,2,1,0:T(8,128)(2,1)}, u32[]{:S(2)}) copy-start(bf16[16,1,128,128]{3,2,1,0:T(8,128)(2,1)} %param.16) | copy-start | bytes 1572868
  3.9 1.0 %copy-start.3 = (bf16[16,1,128,128]{3,2,1,0:T(8,128)(2,1)S(1)}, bf16[16,1,128,128]{3,2,1,0:T(8,128)(2,1)}, u32[]{:S(2)}) copy-start(bf16[16,1,128,128]{3,2,1,0:T(8,128)(2,1)} %param.17) | copy-start | bytes 1572868
  4.9 0.9 %copy-start.4 = (bf16[10,8,4,128]{3,2,1,0:T(4,128)(2,1)S(1)}, bf16[10,8,4,128]{3,2,1,0:T(4,128)(2,1)}, u32[]{:S(2)}) copy-start(bf16[10,8,4,128]{3,2,1,0:T(4,128)(2,1)} %param.18) | copy-start | bytes 245764
  5.8 0.8 %copy-start.5 = (s32[64,64]{1,0:T(8,128)S(1)}, s32[64,64]{1,0:T(8,128)}, u32[]{:S(2)}) copy-start(s32[64,64]{1,0:T(8,128)} %page_source.1) | copy-start | bytes 49156
  6.5 0.8 %copy-start.6 = (s32[64,64]{1,0:T(8,128)S(1)}, s32[64,64]{1,0:T(8,128)}, u32[]{:S(2)}) copy-start(s32[64,64]{1,0:T(8,128)} %page_index.1) | copy-start | bytes 49156
  7.3 0.7 %copy-start.7 = (bf16[10,1,4,128]{3,2,1,0:T(4,128)(2,1)S(1)}, bf16[10,1,4,128]{3,2,1,0:T(4,128)(2,1)}, u32[]{:S(2)}) copy-start(bf16[10,1,4,128]{3,2,1,0:T(4,128)(2,1)} %param.19) | copy-start | bytes 30724
  8.0 0.7 %copy-start.8 = (bf16[10,1,4,128]{3,2,1,0:T(4,128)(2,1)S(1)}, bf16[10,1,4,128]{3,2,1,0:T(4,128)(2,1)}, u32[]{:S(2)}) copy-start(bf16[10,1,4,128]{3,2,1,0:T(4,128)(2,1)} %param.20) | copy-start | bytes 30724
  8.7 0.7 %copy-start.9 = (s32[384]{0:T(512)S(1)}, s32[384]{0:T(512)}, u32[]{:S(2)}) copy-start(s32[384]{0:T(512)} %res_len.1) | copy-start | bytes 4612
  9.4 0.7 %copy-start.10 = (s32[256]{0:T(256)S(1)}, s32[256]{0:T(256)}, u32[]{:S(2)}) copy-start(s32[256]{0:T(256)} %new_len.1) | copy-start | bytes 3076
  10.1 0.7 %copy-start.11 = (s32[64]{0:T(128)S(1)}, s32[64]{0:T(128)}, u32[]{:S(2)}) copy-start(s32[64]{0:T(128)} %partner_bit.1) | copy-start | bytes 772
  10.7 0.7 %copy-start.12 = (s32[64]{0:T(128)S(1)}, s32[64]{0:T(128)}, u32[]{:S(2)}) copy-start(s32[64]{0:T(128)} %migrate_out.1) | copy-start | bytes 772

commit v2 on v1

--- a/solution.py
+++ b/solution.py
@@ -18,7 +18,6 @@
 PAGE = 128
 NPAGES = 16
 LOW = -1e30
-GROUPS = 12
 NT = (((1,), (1,)), ((), ()))
 NN = (((1,), (0,)), ((), ()))
 
@@ -37,6 +36,21 @@
 
 
 def kernel(
+    res_len_in,
+    new_len_in,
+    partner_bit_in,
+    migrate_out_in,
+    page_source_in,
+    page_index_in,
+    queries_in,
+    new_keys_in,
+    new_values_in,
+    res_keys,
+    res_values,
+    pool_keys,
+    pool_values,
+    weight,
+    out,
     res_len,
     new_len,
     partner_bit,
@@ -46,12 +60,6 @@
     queries,
     new_keys,
     new_values,
-    res_keys,
-    res_values,
-    pool_keys,
-    pool_values,
-    weight,
-    out,
     rk,
     rv,
     pk,
@@ -149,11 +157,20 @@
                 (pool_keys, pk),
                 (pool_values, pv),
                 (weight, wv),
+                (page_source_in, page_source),
+                (page_index_in, page_index),
+                (queries_in, queries),
+                (new_keys_in, new_keys),
+                (new_values_in, new_values),
+                (res_len_in, res_len),
+                (new_len_in, new_len),
+                (partner_bit_in, partner_bit),
+                (migrate_out_in, migrate_out),
             ]
         )
     ]
-    for copy in loads:
-        copy.start()
+    for k in (5, 6, 7, 11, 10, 8, 9, 12, 13, 0, 1, 2, 3, 4):
+        loads[k].start()
 
     barrier = pltpu.get_barrier_semaphore()
     for zi in range(1, NZ):
@@ -162,24 +179,8 @@
         pl.semaphore_signal(barrier, inc=1, device_id=(plane(r, z), tp), device_id_type=MESH)
     for o in range(1, TP):
         pl.semaphore_signal(barrier, inc=1, device_id=(me, tp_peer(o)), device_id_type=MESH)
-    pl.semaphore_wait(barrier, NZ - 1 + PEERS - 1 + TP - 1)
-
-    seq = [0, 1, 7, 2, 6, 3, 5, 4]
-    q1_copies = []
-    for i in range(1, NZ):
-        zi = seq[i]
-        back = seq.index(NZ - zi)
-        copy = remote(
-            queries.at[pl.ds(RES * ROWS, NEW * ROWS)],
-            q1.at[back],
-            q1_send.at[i],
-            q1_recv.at[back],
-            line(zi),
-        )
-        copy.start()
-        q1_copies.append(copy)
-    q1[0] = queries[RES * ROWS :, :]
-
+    loads[5].wait()
+    loads[6].wait()
     places = page_source.shape[1]
     count = page_source.shape[0]
     source = page_source[...]
@@ -199,9 +200,27 @@
                 page = jnp.max(jnp.where(place == p, slot, 0), axis=1, keepdims=True)
                 table = jnp.where(lane == 2 * PEERS + c, page, table)
     tab_v[...] = table
-    tab_copy = pltpu.make_async_copy(tab_v, tab, load_sem.at[5])
+    tab_copy = pltpu.make_async_copy(tab_v, tab, load_sem.at[14])
     tab_copy.start()
-    tab_copy.wait()
+
+    pl.semaphore_wait(barrier, NZ - 1 + PEERS - 1 + TP - 1)
+
+    seq = [0, 1, 7, 2, 6, 3, 5, 4]
+    q1_copies = []
+    loads[7].wait()
+    for i in range(1, NZ):
+        zi = seq[i]
+        back = seq.index(NZ - zi)
+        copy = remote(
+            queries.at[pl.ds(RES * ROWS, NEW * ROWS)],
+            q1.at[back],
+            q1_send.at[i],
+            q1_recv.at[back],
+            line(zi),
+        )
+        copy.start()
+        q1_copies.append(copy)
+    q1[0] = queries[RES * ROWS :, :]
 
     def forward(i):
         dest = line(order(i))
@@ -223,6 +242,7 @@
                     fw.at[i, r], q2.at[i, mirror(r)], q2_send.at[i], q2_recv.at[i], plane(r, z)
                 ).start()
 
+    tab_copy.wait()
     forward(jnp.int32(0))
 
     def forward_step(i, carry):
@@ -232,6 +252,8 @@
 
     lax.fori_loop(1, NZ, forward_step, 0)
 
+    for k in range(8, 14):
+        loads[k].wait()
     fresh_count = new_keys.shape[0]
     fresh_k = new_keys[...]
     fresh_v = new_values[...]
@@ -253,10 +275,8 @@
         m = jnp.max(s, axis=1, keepdims=True)
         p = jnp.exp(s - m)
         l = jnp.sum(p, axis=1, keepdims=True)
-        fin[n, 8] = (dot(p.astype(jnp.bfloat16), fresh_v) / l).astype(jnp.bfloat16)
-        for g in range(9, GROUPS):
-            fin[n, g] = jnp.zeros((ROWS, HD), jnp.bfloat16)
-        lf[NZ, pl.ds(n, 1), :] = jnp.where(quarter == 0, as_row(m + jnp.log(l)), LOW)
+        fin[n, 0] = (dot(p.astype(jnp.bfloat16), fresh_v) / l).astype(jnp.bfloat16)
+        lf[0, pl.ds(n, 1), :] = as_row(m + jnp.log(l))
 
     loads[0].wait()
     loads[1].wait()
@@ -304,7 +324,17 @@
     tile_row = iota((2 * NEW, HD), 0)
     key_lane = iota((ROWS, PAGE), 1)
 
-    def partial_step(ip, carry):
+    def send_part(i, r):
+        remote(
+            r1s.at[i, r], r1.at[i, mirror(r)], r1_send.at[i], r1_recv.at[i], plane(r, z)
+        ).start()
+
+    def send_level(ip, r):
+        remote(
+            sts.at[ip, r], st.at[ip, mirror(r)], st_send.at[ip], st_recv.at[ip], plane(r, z)
+        ).start()
+
+    def partial_pair(ip, send):
         tiles = [jnp.full((2 * NEW, HD), LOW, jnp.float32) for _ in range(PEERS)]
         for half in range(2):
             i = 2 * ip + half
@@ -342,29 +372,27 @@
                     wanted = jnp.where(low_half, request[2 * k], request[2 * k + 1]) + half * NEW
                     filled = jnp.where(low_half, request[2 * k], request[2 * k + 1]) < NEW
                     tiles[r] = jnp.where((tile_row == wanted) & filled, level, tiles[r])
-                    if r > 0:
-                        remote(
-                            r1s.at[i, r],
-                            r1.at[i, mirror(r)],
-                            r1_send.at[i],
-                            r1_recv.at[i],
-                            plane(r, z),
-                        ).start()
+                    if r > 0 and send:
+                        send_part(i, r)
         for r in range(PEERS):
             if r == 0:
                 st[ip, 0] = tiles[0]
             else:
                 sts[ip, r] = tiles[r]
-                remote(
-                    sts.at[ip, r],
-                    st.at[ip, mirror(r)],
-                    st_send.at[ip],
-                    st_recv.at[ip],
-                    plane(r, z),
-                ).start()
+                if send:
+                    send_level(ip, r)
+
+    def partial_step(ip, carry):
+        partial_pair(ip, True)
         return carry
 
-    lax.fori_loop(0, NZ // 2, partial_step, 0)
+    partial_pair(jnp.int32(0), False)
+    lax.fori_loop(1, NZ // 2, partial_step, 0)
+    for r in range(1, PEERS):
+        send_level(0, r)
+    for i in (1, 0):
+        for r in range(1, PEERS):
+            send_part(i, r)
 
     for copy in mig_copies:
         copy.wait()
@@ -421,23 +449,30 @@
 
     low = iota((2 * NEW, HD), 1) < 2 * ROWS
 
-    def merge(ip, home):
+    def pair_levels(ip):
         drain(st.at[ip, pl.ds(1, PEERS - 1)], st_recv.at[ip])
-        levels = [
+        return [
             jnp.where(low, st[ip, 2 * q], st[ip, 2 * q + 1]) for q in range(PEERS // 2)
         ]
-        m = jnp.maximum(
-            jnp.maximum(levels[0], levels[1]), jnp.maximum(levels[2], levels[3])
-        )
+
+    def softmax_over(levels):
+        m = levels[0]
+        for level in levels[1:]:
+            m = jnp.maximum(m, level)
         m = jnp.maximum(m, pltpu.roll(m, 2 * ROWS, 1))
         m = jnp.maximum(m, pltpu.roll(m, ROWS, 1))
         shares = [jnp.exp(level - m) for level in levels]
-        total = (shares[0] + shares[1]) + (shares[2] + shares[3])
+        total = shares[0]
+        for share in shares[1:]:
+            total = total + share
         total = total + pltpu.roll(total, 2 * ROWS, 1)
         total = total + pltpu.roll(total, ROWS, 1)
-        ls[ip] = m + jnp.log(total)
-        shares = [share / total for share in shares]
-        for half in range(2):
+        return [share / total for share in shares], m + jnp.log(total)
+
+    def merge(ip, levels, halves):
+        shares, together = softmax_over(levels)
+        ls[ip] = together
+        for half in halves:
             i = 2 * ip + half
             drain(r1.at[i, pl.ds(1, PEERS - 1)], r1_recv.at[i])
             blocks = []
@@ -450,34 +485,29 @@
                 )
             mix = jnp.concatenate(blocks, axis=0).astype(jnp.bfloat16)
             merged = dot(mix, r1[i].reshape(PEERS * 2 * ROWS, HD)).astype(jnp.bfloat16)
-            if home and half == 0:
-                for n in range(NEW):
-                    fin[n, 0] = merged[n * ROWS : (n + 1) * ROWS]
-                lf[0] = ls[ip]
-            else:
-                for n in range(NEW):
-                    r2s[i, n] = merged[n * ROWS : (n + 1) * ROWS]
-                zi = order(i)
-                turned = i + 1 - 2 * lax.rem(i + 1, 2)
-                back = turned - lax.div(turned, NZ)
-                remote(
-                    r2s.at[i], fin.at[:, back], r2_send.at[i], r2_recv.at[back], line(zi)
-                ).start()
-                remote(ls.at[ip], lf.at[back], lf_send.at[i], lf_recv.at[back], line(zi)).start()
-
-    merge(jnp.int32(0), True)
+            for n in range(NEW):
+                r2s[i, n] = merged[n * ROWS : (n + 1) * ROWS]
+            zi = order(i)
+            turned = i + 1 - 2 * lax.rem(i + 1, 2)
+            back = turned - lax.div(turned, NZ)
+            remote(
+                r2s.at[i], fin.at[:, back], r2_send.at[i], r2_recv.at[back], line(zi)
+            ).start()
+            remote(ls.at[ip], lf.at[back], lf_send.at[i], lf_recv.at[back], line(zi)).start()
 
     def merge_step(ip, carry):
-        merge(ip, False)
+        merge(ip, pair_levels(ip), (0, 1))
         return carry
 
     lax.fori_loop(1, NZ // 2, merge_step, 0)
+    near = pair_levels(0)
+    merge(jnp.int32(0), near, (1,))
 
     for i in range(1, NZ):
         drain(lf.at[i], lf_recv.at[i])
         drain(fin.at[:, i], r2_recv.at[i])
     from_odd = [False, False, True, False, True, False, True, True]
-    levels = []
+    levels = [level[:NEW] for level in near]
     for base in range(0, NZ, 4):
         level = jnp.full((NEW, HD), LOW, jnp.float32)
         for g in range(4):
@@ -485,25 +515,38 @@
             rows = lf[i, pl.ds(NEW if from_odd[i] else 0, NEW), :]
             level = jnp.where(quarter == g, rows, level)
         levels.append(level)
-    levels.append(lf[NZ, pl.ds(0, NEW), :])
-    m = jnp.maximum(jnp.maximum(levels[0], levels[1]), levels[2])
-    m = jnp.maximum(m, pltpu.roll(m, 2 * ROWS, 1))
-    m = jnp.maximum(m, pltpu.roll(m, ROWS, 1))
-    shares = [jnp.exp(level - m) for level in levels]
-    total = shares[0] + shares[1] + shares[2]
-    total = total + pltpu.roll(total, 2 * ROWS, 1)
-    total = total + pltpu.roll(total, ROWS, 1)
-    shares = [share / total for share in shares]
-    attended = []
+    shares, _ = softmax_over(levels)
+    tail = NEW * STEPS
+    row = iota((tail, HD), 0)
+    spread = []
+    for share in shares:
+        wide = jnp.zeros((tail, HD), jnp.float32)
+        for n in range(NEW):
+            wide = jnp.where(lax.div(row, STEPS) == n, share[n : n + 1], wide)
+        spread.append(wide)
+    column = lax.rem(iota((tail, HD), 1), ROWS) - lax.rem(row, STEPS)
+    owner = lax.div(row, STEPS)
+
+    def mixing(parts, n):
+        rows = []
+        for h in range(ROWS // STEPS):
+            keep = column == h * STEPS
+            if n is not None:
+                keep = keep & (owner == n)
+            rows.append(
+                jnp.concatenate([jnp.where(keep, part, 0.0) for part in parts], axis=1)
+            )
+        return jnp.concatenate(rows, axis=0).astype(jnp.bfloat16)
+
+    drain(r1.at[0, pl.ds(1, PEERS - 1)], r1_recv.at[0])
+    attended = dot(mixing(spread[: PEERS // 2], None), r1[0].reshape(PEERS * 2 * ROWS, HD))
     for n in range(NEW):
-        mix = jnp.concatenate(
-            [jnp.where(diag, share[n : n + 1], 0.0) for share in shares], axis=1
-        ).astype(jnp.bfloat16)
-        attended.append(dot(mix, fin[n].reshape(GROUPS * ROWS, HD)))
-    moved = by_head(jnp.concatenate(attended, axis=0).astype(jnp.bfloat16), NEW)
-    tail = NEW * STEPS
+        attended = attended + dot(
+            mixing(spread[PEERS // 2 :], n), fin[n].reshape(NZ * ROWS, HD)
+        )
+    attended = attended.astype(jnp.bfloat16)
     for h in range(ROWS // STEPS):
-        xnew[:, pl.ds(h * HD, HD)] = moved[h * tail : (h + 1) * tail]
+        xnew[:, pl.ds(h * HD, HD)] = attended[h * tail : (h + 1) * tail]
     rs2_copies = project(xnew, rs2s, rs2_send, rs2, rs2_recv, own2)
 
     for copy in rs1_copies:
@@ -550,12 +593,22 @@
     rows = (RES + MIG + NEW) * STEPS
     lead, tail = (RES + MIG) * STEPS, NEW * STEPS
     width = out_weight.shape[1] // TP
-    smem = pl.BlockSpec(memory_space=pltpu.SMEM)
     vmem = pl.BlockSpec(memory_space=pltpu.VMEM)
-    hbm = pl.BlockSpec(memory_space=pl.ANY)
+    hbm = pl.BlockSpec(memory_space=pltpu.HBM)
     dma = pltpu.SemaphoreType.DMA
     depth = out_weight.shape[0]
-    scratch = [
+    whole = [
+        pltpu.SMEM(res_len.shape, jnp.int32),
+        pltpu.SMEM(new_len.shape, jnp.int32),
+        pltpu.SMEM(partner_bit.shape, jnp.int32),
+        pltpu.SMEM(migrate_out.shape, jnp.int32),
+        pltpu.VMEM(page_source.shape, jnp.int32),
+        pltpu.VMEM(page_index.shape, jnp.int32),
+        pltpu.VMEM((queries.shape[0] * ROWS, HD), bf),
+        pltpu.VMEM((queries.shape[0] * STEPS, HD), bf),
+        pltpu.VMEM((queries.shape[0] * STEPS, HD), bf),
+    ]
+    scratch = whole + [
         pltpu.VMEM((RES, res_keys.shape[2], HD), bf),
         pltpu.VMEM((RES, res_keys.shape[2], HD), bf),
         pltpu.VMEM((pool_keys.shape[0], PAGE, HD), bf),
@@ -572,8 +625,8 @@
         pltpu.VMEM((NZ // 2, PEERS, 2 * NEW, HD), f32),
         pltpu.VMEM((NZ, NEW, ROWS, HD), bf),
         pltpu.VMEM((NZ // 2, 2 * NEW, HD), f32),
-        pltpu.VMEM((NEW, GROUPS, ROWS, HD), bf),
-        pltpu.VMEM((NZ + 1, 2 * NEW, HD), f32),
+        pltpu.VMEM((NEW, NZ, ROWS, HD), bf),
+        pltpu.VMEM((NZ, 2 * NEW, HD), f32),
         pltpu.VMEM((RES * ROWS, HD), bf),
         pltpu.VMEM((2, MIG * ROWS, HD), bf),
         pltpu.VMEM(((RES + MIG) * ROWS, HD), bf),
@@ -585,7 +638,7 @@
         pltpu.VMEM((TP, lead, width), bf),
         pltpu.VMEM((TP, tail, width), bf),
         pltpu.VMEM((TP, tail, width), bf),
-        dma((6,)),
+        dma((15,)),
         dma((NZ,)),
         dma((NZ,)),
         dma((NZ,)),
@@ -608,11 +661,11 @@
     return pl.pallas_call(
         kernel,
         out_shape=jax.ShapeDtypeStruct((rows, width), bf),
-        in_specs=[smem] * 4 + [vmem] * 5 + [hbm] * 5,
+        in_specs=[hbm] * 14,
         out_specs=vmem,
         scratch_shapes=scratch,
         compiler_params=pltpu.CompilerParams(
-            collective_id=0, has_side_effects=True, vmem_limit_bytes=48 * 2**20
+            collective_id=0, has_side_effects=True, vmem_limit_bytes=64 * 2**20
         ),
         cost_estimate=pl.CostEstimate(
             flops=10**9, bytes_accessed=16 * 2**20, transcendentals=10**6

time: 65.3 us -> 54 us (0.83)
  local copies, waits for them, and re-layouts: 12 us -> 1.54 us
    unnamed x27 -> x1, local copies, waits for them, and re-layouts: 12 us -> 1.54 us
where the time goes in v2:
time: 54 us; the launch traced here: 53.9 us
  Pallas kernels  52.4 us (97%)
  local copies, waits for them, and re-layouts  1.54 us (3%)
    pallas_call x1, Pallas kernels, per_device(): pl.pallas_call(kernel, out_shape=jax.ShapeDtypeStruct((rows, width), bf),...  52.4 us
    unnamed x1, local copies, waits for them, and re-layouts  1.54 us

profile of v2, /device:TPU:1, one launch (start us, length us, event | category | flops | bytes accessed | tf_op | source)
XLA Modules:
  0.0 53.9 jit_solution(2884042817506635594)
XLA Ops:
  0.0 52.4 %shard_map.136 = bf16[48,1024]{1,0:T(8,128)(2,1)} custom-call(s32[384]{0:T(512)} %res_len_in.1, s32[256]{0:T(256)} %new_len_in.1, s32[64]{0:T(128)} %partner_bit_in.1, s32[64]{0:T(128)} %migrate_out_in.1, s32[64,64]{1,0:T(8,128)} %page_source_in.1, s32[64,64]{1,0:T(8,128)} %page_index_in.1, bf16[320,128]{1,0:T(8,128)(2,1)} %bitcast.11, ...), custom_call_target="tpu_custom_call" | custom-call | flops 1000000000 | bytes 16777216 | tf_op jit(solution)/shard_map/pallas_call | solution.py:661
  52.4 1.5 %copy.16 = bf16[48,1024]{1,0:T(8,128)(2,1)} copy(bf16[48,1024]{1,0:T(8,128)(2,1)} %shard_map.136) | data formatting | bytes 196608

commit v3 on v2

--- a/solution.py
+++ b/solution.py
@@ -128,6 +128,9 @@
     def line(zi):
         return inst_at(x, lax.rem(z + zi, NZ), y)
 
+    bases = [plane(r, 0) for r in range(PEERS)]
+    peers = [base + z * NY for base in bases]
+
     def tp_peer(o):
         return lax.rem(hi + o // 2, 2) * 2 + lax.rem(core + o % 2, 2)
 
@@ -176,7 +179,7 @@
     for zi in range(1, NZ):
         pl.semaphore_signal(barrier, inc=1, device_id=(line(zi), tp), device_id_type=MESH)
     for r in range(1, PEERS):
-        pl.semaphore_signal(barrier, inc=1, device_id=(plane(r, z), tp), device_id_type=MESH)
+        pl.semaphore_signal(barrier, inc=1, device_id=(peers[r], tp), device_id_type=MESH)
     for o in range(1, TP):
         pl.semaphore_signal(barrier, inc=1, device_id=(me, tp_peer(o)), device_id_type=MESH)
     loads[5].wait()
@@ -189,16 +192,17 @@
     lane = iota((count, HD), 1)
     table = jnp.zeros((count, HD), jnp.int32)
     for r in range(PEERS):
-        hit = source == plane(r, z)
+        hit = source == peers[r]
         first = jnp.min(jnp.where(hit, place, places), axis=1, keepdims=True)
         last = jnp.max(jnp.where(hit, place, -1), axis=1, keepdims=True)
         last = jnp.where(last > first, last, places)
-        table = jnp.where(lane == 2 * r, first, table)
-        table = jnp.where(lane == 2 * r + 1, last, table)
-        if r == 0:
-            for c, p in ((0, first), (1, last)):
+        for c, p in ((0, first), (1, last)):
+            table = jnp.where(lane == 2 * r + c, lax.shift_right_logical(p, NPAGES.bit_length() - 1), table)
+            if r == 0:
                 page = jnp.max(jnp.where(place == p, slot, 0), axis=1, keepdims=True)
                 table = jnp.where(lane == 2 * PEERS + c, page, table)
+                skip = (p & (NPAGES - 1)) * PAGE
+                table = jnp.where(lane == 2 * PEERS + 2 + c, skip, table)
     tab_v[...] = table
     tab_copy = pltpu.make_async_copy(tab_v, tab, load_sem.at[14])
     tab_copy.start()
@@ -227,7 +231,7 @@
         block = [q1[i, pl.ds(n * ROWS, ROWS), :] for n in range(NEW)]
         for r in range(PEERS):
             for c in range(2):
-                n = lax.div(tab[dest, 2 * r + c], NPAGES)
+                n = tab[dest, 2 * r + c]
                 q = lax.select(
                     n == 0,
                     block[0],
@@ -239,7 +243,7 @@
                     fw[i, r, pl.ds(c * ROWS, ROWS), :] = q
             if r > 0:
                 remote(
-                    fw.at[i, r], q2.at[i, mirror(r)], q2_send.at[i], q2_recv.at[i], plane(r, z)
+                    fw.at[i, r], q2.at[i, mirror(r)], q2_send.at[i], q2_recv.at[i], peers[r]
                 ).start()
 
     tab_copy.wait()
@@ -326,30 +330,29 @@
 
     def send_part(i, r):
         remote(
-            r1s.at[i, r], r1.at[i, mirror(r)], r1_send.at[i], r1_recv.at[i], plane(r, z)
+            r1s.at[i, r], r1.at[i, mirror(r)], r1_send.at[i], r1_recv.at[i], peers[r]
         ).start()
 
     def send_level(ip, r):
         remote(
-            sts.at[ip, r], st.at[ip, mirror(r)], st_send.at[ip], st_recv.at[ip], plane(r, z)
+            sts.at[ip, r], st.at[ip, mirror(r)], st_send.at[ip], st_recv.at[ip], peers[r]
         ).start()
 
-    def partial_pair(ip, send):
+    def partial_pair(ip, send, halves=(0, 1)):
         tiles = [jnp.full((2 * NEW, HD), LOW, jnp.float32) for _ in range(PEERS)]
-        for half in range(2):
+        for half in halves:
             i = 2 * ip + half
             drain(q2.at[i, pl.ds(1, PEERS - 1)], q2_recv.at[i])
             dest_z = lax.rem(z + order(i), NZ)
-            for base in range(0, PEERS, 2):
+            for base in range(0, PEERS, 8):
                 scores, values, request = [], [], []
-                for r in (base, base + 1):
-                    dest = plane(r, dest_z)
+                for r in range(base, base + 8):
+                    dest = bases[r] + dest_z * NY
                     for c in range(2):
-                        at = tab[dest, c]
+                        n = tab[dest, c]
                         page = tab[dest, 2 * PEERS + c]
-                        n = lax.div(at, NPAGES)
                         length = new_len[dest * NEW + jnp.minimum(n, NEW - 1)]
-                        live = length - lax.rem(at, NPAGES) * PAGE
+                        live = length - tab[dest, 2 * PEERS + 2 + c]
                         s = dot(q2[i, r, pl.ds(c * ROWS, ROWS), :], pk[page], NT) * scale
                         scores.append(jnp.where(key_lane < live, s, LOW))
                         values.append(pv[page])
@@ -362,7 +365,7 @@
                     for p, v, l in zip(exps, values, sums)
                 ]
                 rows = [as_row(m + jnp.log(l)) for m, l in zip(tops, sums)]
-                for k, r in enumerate((base, base + 1)):
+                for k, r in enumerate(range(base, base + 8)):
                     for c in range(2):
                         if r == 0:
                             r1[i, 0, pl.ds(c * ROWS, ROWS), :] = outs[2 * k + c]
@@ -386,13 +389,8 @@
         partial_pair(ip, True)
         return carry
 
-    partial_pair(jnp.int32(0), False)
     lax.fori_loop(1, NZ // 2, partial_step, 0)
-    for r in range(1, PEERS):
-        send_level(0, r)
-    for i in (1, 0):
-        for r in range(1, PEERS):
-            send_part(i, r)
+    partial_pair(jnp.int32(0), True, (1, 0))
 
     for copy in mig_copies:
         copy.wait()
@@ -503,6 +501,7 @@
     near = pair_levels(0)
     merge(jnp.int32(0), near, (1,))
 
+    drain(r1.at[0, pl.ds(1, PEERS - 1)], r1_recv.at[0])
     for i in range(1, NZ):
         drain(lf.at[i], lf_recv.at[i])
         drain(fin.at[:, i], r2_recv.at[i])
@@ -538,7 +537,6 @@
             )
         return jnp.concatenate(rows, axis=0).astype(jnp.bfloat16)
 
-    drain(r1.at[0, pl.ds(1, PEERS - 1)], r1_recv.at[0])
     attended = dot(mixing(spread[: PEERS // 2], None), r1[0].reshape(PEERS * 2 * ROWS, HD))
     for n in range(NEW):
         attended = attended + dot(
@@ -665,26 +663,31 @@
         out_specs=vmem,
         scratch_shapes=scratch,
         compiler_params=pltpu.CompilerParams(
-            collective_id=0, has_side_effects=True, vmem_limit_bytes=64 * 2**20
+            collective_id=0, has_side_effects=True, vmem_limit_bytes=48 * 2**20
         ),
         cost_estimate=pl.CostEstimate(
             flops=10**9, bytes_accessed=16 * 2**20, transcendentals=10**6
         ),
     )(
-        res_len,
-        new_len,
-        partner_bit,
-        migrate_out,
-        page_source,
-        page_index,
-        queries.reshape(-1, HD),
-        new_keys.reshape(-1, HD),
-        new_values.reshape(-1, HD),
-        res_keys.reshape(RES, -1, HD),
-        res_values.reshape(RES, -1, HD),
-        pool_keys.reshape(-1, PAGE, HD),
-        pool_values.reshape(-1, PAGE, HD),
-        out_weight,
+        *(
+            pltpu.with_memory_space_constraint(operand, pltpu.HBM)
+            for operand in (
+                res_len,
+                new_len,
+                partner_bit,
+                migrate_out,
+                page_source,
+                page_index,
+                queries.reshape(-1, HD),
+                new_keys.reshape(-1, HD),
+                new_values.reshape(-1, HD),
+                res_keys.reshape(RES, -1, HD),
+                res_values.reshape(RES, -1, HD),
+                pool_keys.reshape(-1, PAGE, HD),
+                pool_values.reshape(-1, PAGE, HD),
+                out_weight,
+            )
+        )
     )
 
 

time: 54 us -> 50 us (0.926)
  Pallas kernels: 52.4 us -> 49.3 us
  local copies, waits for them, and re-layouts: 1.54 us -> 0.64 us
    pallas_call x1, Pallas kernels: 52.4 us -> 49.3 us  [per_device(): pl.pallas_call(kernel, out_shape=jax.ShapeDtypeStruct((rows, width), bf),...]
    unnamed x1, local copies, waits for them, and re-layouts: 1.54 us -> 0.64 us
where the time goes in v3:
time: 50 us; the launch traced here: 49.9 us
  Pallas kernels  49.3 us (99%)
  local copies, waits for them, and re-layouts  0.64 us (1%)
    pallas_call x1, Pallas kernels, per_device(): pl.pallas_call(kernel, out_shape=jax.ShapeDtypeStruct((rows, width), bf),...  49.3 us

profile of v3, /device:TPU:1, one launch (start us, length us, event | category | flops | bytes accessed | tf_op | source)
XLA Modules:
  0.0 49.9 jit_solution(6395509865049365975)
XLA Ops:
  0.0 49.3 %shard_map.136 = bf16[48,1024]{1,0:T(8,128)(2,1)S(1)} custom-call(s32[384]{0:T(512)} %res_len_in.1, s32[256]{0:T(256)} %new_len_in.1, s32[64]{0:T(128)} %partner_bit_in.1, s32[64]{0:T(128)} %migrate_out_in.1, s32[64,64]{1,0:T(8,128)} %page_source_in.1, s32[64,64]{1,0:T(8,128)} %page_index_in.1, bf16[320,128]{1,0:T(8,128)(2,1)} %bitcast.11, ...), custom_call_target="tpu_custom_call" | custom-call | flops 1000000000 | bytes 16777216 | tf_op jit(solution)/shard_map/pallas_call | solution.py:659
  49.3 0.6 %copy.16 = bf16[48,1024]{1,0:T(8,128)(2,1)} copy(bf16[48,1024]{1,0:T(8,128)(2,1)S(1)} %shard_map.136) | data formatting | bytes 196608

commit v4 on v3

--- a/solution.py
+++ b/solution.py
@@ -333,15 +333,23 @@
             r1s.at[i, r], r1.at[i, mirror(r)], r1_send.at[i], r1_recv.at[i], peers[r]
         ).start()
 
-    def send_level(ip, r):
-        remote(
-            sts.at[ip, r], st.at[ip, mirror(r)], st_send.at[ip], st_recv.at[ip], peers[r]
-        ).start()
-
-    def partial_pair(ip, send, halves=(0, 1)):
+    def send_level(tile):
+        for r in range(1, PEERS):
+            remote(
+                sts.at[tile, r],
+                st.at[tile, mirror(r)],
+                st_send.at[tile],
+                st_recv.at[tile],
+                peers[r],
+            ).start()
+
+    tile_of = {1: (0, 0), 2: (0, 1), 3: (1, 0), 0: (1, 1)}
+    low = iota((2 * NEW, HD), 1) < 2 * ROWS
+
+    def partial_pair(ip, halves=(0, 1)):
         tiles = [jnp.full((2 * NEW, HD), LOW, jnp.float32) for _ in range(PEERS)]
         for half in halves:
-            i = 2 * ip + half
+            i = jnp.int32(2 * ip + half)
             drain(q2.at[i, pl.ds(1, PEERS - 1)], q2_recv.at[i])
             dest_z = lax.rem(z + order(i), NZ)
             for base in range(0, PEERS, 8):
@@ -375,22 +383,21 @@
                     wanted = jnp.where(low_half, request[2 * k], request[2 * k + 1]) + half * NEW
                     filled = jnp.where(low_half, request[2 * k], request[2 * k + 1]) < NEW
                     tiles[r] = jnp.where((tile_row == wanted) & filled, level, tiles[r])
-                    if r > 0 and send:
+                    if r > 0:
                         send_part(i, r)
+        tile, second = tile_of[ip]
         for r in range(PEERS):
-            if r == 0:
-                st[ip, 0] = tiles[0]
+            into = sts if r > 0 else st
+            if second:
+                into[tile, r] = jnp.where(low, into[tile, r], tiles[r])
             else:
-                sts[ip, r] = tiles[r]
-                if send:
-                    send_level(ip, r)
-
-    def partial_step(ip, carry):
-        partial_pair(ip, True)
-        return carry
-
-    lax.fori_loop(1, NZ // 2, partial_step, 0)
-    partial_pair(jnp.int32(0), True, (1, 0))
+                into[tile, r] = tiles[r]
+        if second:
+            send_level(tile)
+
+    for ip in (1, 2, 3):
+        partial_pair(ip)
+    partial_pair(0, (1, 0))
 
     for copy in mig_copies:
         copy.wait()
@@ -445,13 +452,17 @@
 
     rs1_copies = project(xres, rs1s, rs1_send, rs1, rs1_recv, own1)
 
-    low = iota((2 * NEW, HD), 1) < 2 * ROWS
-
     def pair_levels(ip):
-        drain(st.at[ip, pl.ds(1, PEERS - 1)], st_recv.at[ip])
-        return [
-            jnp.where(low, st[ip, 2 * q], st[ip, 2 * q + 1]) for q in range(PEERS // 2)
-        ]
+        tile, second = tile_of[ip]
+        levels = []
+        for q in range(0, PEERS, 2):
+            left, right = st[tile, q], st[tile, q + 1]
+            if second:
+                left = pltpu.roll(left, 2 * ROWS, 1)
+            else:
+                right = pltpu.roll(right, 2 * ROWS, 1)
+            levels.append(jnp.where(low, left, right))
+        return levels
 
     def softmax_over(levels):
         m = levels[0]
@@ -493,11 +504,11 @@
             ).start()
             remote(ls.at[ip], lf.at[back], lf_send.at[i], lf_recv.at[back], line(zi)).start()
 
-    def merge_step(ip, carry):
-        merge(ip, pair_levels(ip), (0, 1))
-        return carry
-
-    lax.fori_loop(1, NZ // 2, merge_step, 0)
+    for ip in (1, 2, 3):
+        if ip != 2:
+            tile = tile_of[ip][0]
+            drain(st.at[tile, pl.ds(1, PEERS - 1)], st_recv.at[tile])
+        merge(jnp.int32(ip), pair_levels(ip), (0, 1))
     near = pair_levels(0)
     merge(jnp.int32(0), near, (1,))
 
@@ -561,8 +572,8 @@
         if i > 0:
             drain(r2s.at[i], r2_send.at[i])
             drain(ls.at[i // 2], lf_send.at[i])
-    for ip in range(NZ // 2):
-        drain(sts.at[ip, pl.ds(1, PEERS - 1)], st_send.at[ip])
+    for tile in range(2):
+        drain(sts.at[tile, pl.ds(1, PEERS - 1)], st_send.at[tile])
     for copy in rs2_copies:
         copy.wait()
     total = own2[...]
@@ -619,8 +630,8 @@
         pltpu.VMEM((NZ, PEERS, 2 * ROWS, HD), bf),
         pltpu.VMEM((NZ, PEERS, 2 * ROWS, HD), bf),
         pltpu.VMEM((NZ, PEERS, 2 * ROWS, HD), bf),
-        pltpu.VMEM((NZ // 2, PEERS, 2 * NEW, HD), f32),
-        pltpu.VMEM((NZ // 2, PEERS, 2 * NEW, HD), f32),
+        pltpu.VMEM((2, PEERS, 2 * NEW, HD), f32),
+        pltpu.VMEM((2, PEERS, 2 * NEW, HD), f32),
         pltpu.VMEM((NZ, NEW, ROWS, HD), bf),
         pltpu.VMEM((NZ // 2, 2 * NEW, HD), f32),
         pltpu.VMEM((NEW, NZ, ROWS, HD), bf),

time: 50 us -> 50.9 us (1.018)
  Pallas kernels: 49.3 us -> 50.1 us
    pallas_call x1, Pallas kernels: 49.3 us -> 50.1 us  [per_device(): pl.pallas_call(kernel, out_shape=jax.ShapeDtypeStruct((rows, width), bf),...]
where the time goes in v4:
time: 50.9 us; the launch traced here: 50.7 us
  Pallas kernels  50.1 us (98%)
  local copies, waits for them, and re-layouts  0.64 us (1%)
    pallas_call x1, Pallas kernels, per_device(): pl.pallas_call(kernel, out_shape=jax.ShapeDtypeStruct((rows, width), bf),...  50.1 us

profile of v4, /device:TPU:1, one launch (start us, length us, event | category | flops | bytes accessed | tf_op | source)
XLA Modules:
  0.0 50.7 jit_solution(5149650920299550675)
XLA Ops:
  0.0 50.1 %shard_map.136 = bf16[48,1024]{1,0:T(8,128)(2,1)S(1)} custom-call(s32[384]{0:T(512)} %res_len_in.1, s32[256]{0:T(256)} %new_len_in.1, s32[64]{0:T(128)} %partner_bit_in.1, s32[64]{0:T(128)} %migrate_out_in.1, s32[64,64]{1,0:T(8,128)} %page_source_in.1, s32[64,64]{1,0:T(8,128)} %page_index_in.1, bf16[320,128]{1,0:T(8,128)(2,1)} %bitcast.11, ...), custom_call_target="tpu_custom_call" | custom-call | flops 1000000000 | bytes 16777216 | tf_op jit(solution)/shard_map/pallas_call | solution.py:670
  50.1 0.6 %copy.16 = bf16[48,1024]{1,0:T(8,128)(2,1)} copy(bf16[48,1024]{1,0:T(8,128)(2,1)S(1)} %shard_map.136) | data formatting | bytes 196608

commit v5 on v3

--- a/solution.py
+++ b/solution.py
@@ -182,6 +182,22 @@
         pl.semaphore_signal(barrier, inc=1, device_id=(peers[r], tp), device_id_type=MESH)
     for o in range(1, TP):
         pl.semaphore_signal(barrier, inc=1, device_id=(me, tp_peer(o)), device_id_type=MESH)
+    pl.semaphore_wait(barrier, NZ - 1 + PEERS - 1 + TP - 1)
+
+    seq = [0, 1, 7, 2, 6, 3, 5, 4]
+    q1_copies = []
+    for i in range(1, NZ):
+        zi = seq[i]
+        back = seq.index(NZ - zi)
+        copy = remote(
+            queries_in.at[pl.ds(RES * ROWS, NEW * ROWS)],
+            q1.at[back],
+            q1_send.at[i],
+            q1_recv.at[back],
+            line(zi),
+        )
+        copy.start()
+        q1_copies.append(copy)
     loads[5].wait()
     loads[6].wait()
     places = page_source.shape[1]
@@ -207,23 +223,7 @@
     tab_copy = pltpu.make_async_copy(tab_v, tab, load_sem.at[14])
     tab_copy.start()
 
-    pl.semaphore_wait(barrier, NZ - 1 + PEERS - 1 + TP - 1)
-
-    seq = [0, 1, 7, 2, 6, 3, 5, 4]
-    q1_copies = []
     loads[7].wait()
-    for i in range(1, NZ):
-        zi = seq[i]
-        back = seq.index(NZ - zi)
-        copy = remote(
-            queries.at[pl.ds(RES * ROWS, NEW * ROWS)],
-            q1.at[back],
-            q1_send.at[i],
-            q1_recv.at[back],
-            line(zi),
-        )
-        copy.start()
-        q1_copies.append(copy)
     q1[0] = queries[RES * ROWS :, :]
 
     def forward(i):

time: 50 us -> 50.3 us (level)
  no operation moved by 1% of the time
where the time goes in v5:
time: 50.3 us; the launch traced here: 50.2 us
  Pallas kernels  49.5 us (98%)
  local copies, waits for them, and re-layouts  0.64 us (1%)
    pallas_call x1, Pallas kernels, per_device(): pl.pallas_call(kernel, out_shape=jax.ShapeDtypeStruct((rows, width), bf),...  49.5 us

profile of v5, /device:TPU:1, one launch (start us, length us, event | category | flops | bytes accessed | tf_op | source)
XLA Modules:
  0.0 50.2 jit_solution(11635750354196004337)
XLA Ops:
  0.0 49.5 %shard_map.136 = bf16[48,1024]{1,0:T(8,128)(2,1)S(1)} custom-call(s32[384]{0:T(512)} %res_len_in.1, s32[256]{0:T(256)} %new_len_in.1, s32[64]{0:T(128)} %partner_bit_in.1, s32[64]{0:T(128)} %migrate_out_in.1, s32[64,64]{1,0:T(8,128)} %page_source_in.1, s32[64,64]{1,0:T(8,128)} %page_index_in.1, bf16[320,128]{1,0:T(8,128)(2,1)} %bitcast.11, ...), custom_call_target="tpu_custom_call" | custom-call | flops 1000000000 | bytes 16777216 | tf_op jit(solution)/shard_map/pallas_call | solution.py:659
  49.5 0.6 %copy.16 = bf16[48,1024]{1,0:T(8,128)(2,1)} copy(bf16[48,1024]{1,0:T(8,128)(2,1)S(1)} %shard_map.136) | data formatting | bytes 196608

commit v6 on v3

--- a/solution.py
+++ b/solution.py
@@ -375,15 +375,15 @@
                     wanted = jnp.where(low_half, request[2 * k], request[2 * k + 1]) + half * NEW
                     filled = jnp.where(low_half, request[2 * k], request[2 * k + 1]) < NEW
                     tiles[r] = jnp.where((tile_row == wanted) & filled, level, tiles[r])
-                    if r > 0 and send:
+                    if r > 0 and half == halves[0]:
                         send_part(i, r)
         for r in range(PEERS):
             if r == 0:
                 st[ip, 0] = tiles[0]
             else:
                 sts[ip, r] = tiles[r]
-                if send:
-                    send_level(ip, r)
+                send_level(ip, r)
+                send_part(2 * ip + halves[1], r)
 
     def partial_step(ip, carry):
         partial_pair(ip, True)

time: 50 us -> 49.3 us (0.986)
  Pallas kernels: 49.3 us -> 48.6 us
    pallas_call x1, Pallas kernels: 49.3 us -> 48.6 us  [per_device(): pl.pallas_call(kernel, out_shape=jax.ShapeDtypeStruct((rows, width), bf),...]
where the time goes in v6:
time: 49.3 us; the launch traced here: 49.2 us
  Pallas kernels  48.6 us (99%)
  local copies, waits for them, and re-layouts  0.64 us (1%)
    pallas_call x1, Pallas kernels, per_device(): pl.pallas_call(kernel, out_shape=jax.ShapeDtypeStruct((rows, width), bf),...  48.6 us

profile of v6, /device:TPU:1, one launch (start us, length us, event | category | flops | bytes accessed | tf_op | source)
XLA Modules:
  0.0 49.2 jit_solution(4474301479152103092)
XLA Ops:
  0.0 48.6 %shard_map.136 = bf16[48,1024]{1,0:T(8,128)(2,1)S(1)} custom-call(s32[384]{0:T(512)} %res_len_in.1, s32[256]{0:T(256)} %new_len_in.1, s32[64]{0:T(128)} %partner_bit_in.1, s32[64]{0:T(128)} %migrate_out_in.1, s32[64,64]{1,0:T(8,128)} %page_source_in.1, s32[64,64]{1,0:T(8,128)} %page_index_in.1, bf16[320,128]{1,0:T(8,128)(2,1)} %bitcast.11, ...), custom_call_target="tpu_custom_call" | custom-call | flops 1000000000 | bytes 16777216 | tf_op jit(solution)/shard_map/pallas_call | solution.py:659
  48.6 0.6 %copy.16 = bf16[48,1024]{1,0:T(8,128)(2,1)} copy(bf16[48,1024]{1,0:T(8,128)(2,1)S(1)} %shard_map.136) | data formatting | bytes 196608
